TPU v7x, 128 devices: a whole 4x4x4 slice. The times are simulated.
128 devices in a mesh: seq: 16 (over z, x_lo, core), head: 8 (over x_hi, y).
Axes of the slice: x: 4 (x_hi: 2, x_lo: 2; x = x_hi * 2 + x_lo), y: 4, z: 4, core: 2. Of those that a mesh axis runs over, the one named last changes fastest.
Arguments:
- queries: bfloat16 [8192, 8192], P(('seq', 'head')), may hold values from -120 to 120
- keys: bfloat16 [8192, 1024], P(('seq', 'head')), may hold values from -5 to 5
- values: bfloat16 [8192, 1024], P(('seq', 'head')), may hold values from -5 to 5
- out_grad: bfloat16 [8192, 8192], P(('seq', 'head')), may hold values from -5 to 5
- prefix_keys: bfloat16 [256, 1024], P(None, 'head'), may hold values from -4 to 4
- prefix_values: bfloat16 [256, 1024], P(None, 'head'), may hold values from -5 to 5
- seg_ids: int32 [8192], replicated, may hold values from 0 to 31, never falling along the last dimension, each value on 1 to 1024 neighbouring positions
- prefix_lens: int32 [32], replicated, may hold values from 64 to 256, as said below
Outputs:
- query_grad: bfloat16 [8192, 8192], P(('seq', 'head'))
- key_grad: bfloat16 [8192, 1024], P(('seq', 'head'))
- value_grad: bfloat16 [8192, 1024], P(('seq', 'head'))
- prefix_key_grad: bfloat16 [256, 1024], P(None, 'head')
- prefix_value_grad: bfloat16 [256, 1024], P(None, 'head')
Inputs may be any that keep to these rules, and one draw needn't show every extreme that they name: `prefix_lens`: each document sees at least the first 64 prefix tokens; some document sees all 256. `seg_ids`: each document holds at most 1024 tokens; some document holds exactly 1024.
All inputs are finite; a program needn't handle non-finite values.
Results may differ from a plain program's by a relative error of at most 0.0065.
Values may be sent and summed in bfloat16 or wider, within the bound.
A program may use at most 128 MiB of HBM per device.

v0:
```python
import math

import jax
import jax.numpy as jnp
from jax import lax
from jax.sharding import PartitionSpec as P

HEADS = 64
KV_HEADS = 8
HEAD_DIM = 128
PREFIX = 256


masked_score = -1e30


def prefix_limits(seg_rows, prefix_lens):
    labels = jnp.arange(prefix_lens.shape[0], dtype=jnp.int32)
    return jnp.sum(jnp.where(seg_rows[:, None] == labels[None, :], prefix_lens[None, :], 0), axis=1)


def attend_piece(
    query_rows,
    grad_rows,
    row_start,
    prefix_keys,
    prefix_values,
    slab_keys,
    slab_values,
    seg_ids,
    prefix_lens,
):
    row_count = query_rows.shape[0]
    kv_here = prefix_keys.shape[1] // HEAD_DIM
    group_size = HEADS // KV_HEADS
    score_scale = HEAD_DIM ** (-0.5)
    query_split = query_rows.reshape(row_count, kv_here, group_size, HEAD_DIM)
    grad_split = grad_rows.reshape(row_count, kv_here, group_size, HEAD_DIM)
    positions = row_start + jnp.arange(row_count, dtype=jnp.int32)
    seg_rows = lax.dynamic_slice_in_dim(seg_ids, row_start, row_count)
    limits = prefix_limits(seg_rows, prefix_lens)
    prefix_allowed = jnp.arange(PREFIX, dtype=jnp.int32)[None, :] < limits[:, None]
    prefix_key = prefix_keys.reshape(PREFIX, kv_here, HEAD_DIM)
    prefix_value = prefix_values.reshape(PREFIX, kv_here, HEAD_DIM)
    key_count = slab_keys.shape[0]
    doc_longest = min(1024, key_count // 2)
    window_len = min(key_count, doc_longest + row_count)
    window_start = jnp.clip(row_start + row_count - window_len, 0, key_count - window_len)
    block_size = math.gcd(window_len, 512)
    block_count = window_len // block_size
    block_order = jnp.arange(block_count, dtype=jnp.int32)

    def scores(key_block, allowed):
        raw_scores = (
            jnp.einsum("rcge,kce->cgrk", query_split, key_block, preferred_element_type=jnp.float32)
            * score_scale
        )
        return jnp.where(allowed[None, None], raw_scores, masked_score)

    def slab_block(block_index):
        first_key = window_start + block_index * block_size
        key_block = lax.dynamic_slice_in_dim(slab_keys, first_key, block_size).reshape(
            block_size, kv_here, HEAD_DIM
        )
        value_block = lax.dynamic_slice_in_dim(slab_values, first_key, block_size).reshape(
            block_size, kv_here, HEAD_DIM
        )
        key_positions = first_key + jnp.arange(block_size, dtype=jnp.int32)
        key_segments = lax.dynamic_slice_in_dim(seg_ids, first_key, block_size)
        allowed = (seg_rows[:, None] == key_segments[None, :]) & (
            key_positions[None, :] <= positions[:, None]
        )
        return (key_block, value_block, allowed)

    first_scores = scores(prefix_key, prefix_allowed)
    row_peak = jnp.max(first_scores, axis=-1)
    weights = jnp.exp(first_scores - row_peak[..., None])
    value_dots = jnp.einsum(
        "rcge,kce->cgrk", grad_split, prefix_value, preferred_element_type=jnp.float32
    )
    running = (row_peak, jnp.sum(weights, axis=-1), jnp.sum(weights * value_dots, axis=-1))

    def forward_step(running, block_index):
        key_block, value_block, allowed = slab_block(block_index)

        def update(running):
            old_peak, old_totals, old_weighted = running
            block_scores = scores(key_block, allowed)
            new_peak = jnp.maximum(old_peak, jnp.max(block_scores, axis=-1))
            block_weights = jnp.exp(block_scores - new_peak[..., None])
            factor = jnp.exp(old_peak - new_peak)
            block_dots = jnp.einsum(
                "rcge,kce->cgrk", grad_split, value_block, preferred_element_type=jnp.float32
            )
            return (
                new_peak,
                old_totals * factor + jnp.sum(block_weights, axis=-1),
                old_weighted * factor + jnp.sum(block_weights * block_dots, axis=-1),
            )

        def unchanged(running):
            return running

        return (lax.cond(jnp.any(allowed), update, unchanged, running), None)

    (row_peak, row_totals, weighted), _ = lax.scan(forward_step, running, block_order)
    log_totals = row_peak + jnp.log(row_totals)
    row_delta = weighted / row_totals

    def gradients(key_block, value_block, allowed):
        probability = jnp.exp(scores(key_block, allowed) - log_totals[..., None])
        block_dots = jnp.einsum(
            "rcge,kce->cgrk", grad_split, value_block, preferred_element_type=jnp.float32
        )
        score_grad = (probability * (block_dots - row_delta[..., None])).astype(jnp.bfloat16)
        rounded_probs = probability.astype(jnp.bfloat16)
        query_part = jnp.einsum(
            "cgrk,kce->rcge", score_grad, key_block, preferred_element_type=jnp.float32
        )
        key_part = (
            jnp.einsum(
                "cgrk,rcge->kce", score_grad, query_split, preferred_element_type=jnp.float32
            )
            * score_scale
        )
        value_part = jnp.einsum(
            "cgrk,rcge->kce", rounded_probs, grad_split, preferred_element_type=jnp.float32
        )
        return (query_part, key_part, value_part)

    query_total, prefix_kgrad, prefix_vgrad = gradients(prefix_key, prefix_value, prefix_allowed)

    def backward_step(query_total, block_index):
        key_block, value_block, allowed = slab_block(block_index)

        def active(query_total):
            query_part, key_part, value_part = gradients(key_block, value_block, allowed)
            return (query_total + query_part, key_part, value_part)

        def inactive(query_total):
            empty_block = jnp.zeros((block_size, kv_here, HEAD_DIM), jnp.float32)
            return (query_total, empty_block, empty_block)

        query_total, key_part, value_part = lax.cond(
            jnp.any(allowed), active, inactive, query_total
        )
        return (query_total, (key_part, value_part))

    query_total, (key_parts, value_parts) = lax.scan(backward_step, query_total, block_order)
    query_total = (query_total * score_scale).reshape(row_count, kv_here * group_size * HEAD_DIM)
    feature_width = kv_here * HEAD_DIM
    empty_full = jnp.zeros((key_count, feature_width), jnp.float32)
    key_full = lax.dynamic_update_slice_in_dim(
        empty_full, key_parts.reshape(window_len, feature_width), window_start, 0
    )
    value_full = lax.dynamic_update_slice_in_dim(
        empty_full, value_parts.reshape(window_len, feature_width), window_start, 0
    )
    return (
        query_total,
        key_full,
        value_full,
        prefix_kgrad.reshape(PREFIX, feature_width),
        prefix_vgrad.reshape(PREFIX, feature_width),
    )


def on_device(queries, keys, values, out_grad, prefix_keys, prefix_values, seg_ids, prefix_lens):
    seq_index = lax.axis_index("seq")
    query_local, grad_local, key_local, value_local = (
        lax.all_to_all(queries, "head", split_axis=1, concat_axis=0, tiled=True),
        lax.all_to_all(out_grad, "head", split_axis=1, concat_axis=0, tiled=True),
        lax.all_to_all(keys, "head", split_axis=1, concat_axis=0, tiled=True),
        lax.all_to_all(values, "head", split_axis=1, concat_axis=0, tiled=True),
    )
    slab_keys, slab_values = (
        lax.all_gather(key_local, "seq", axis=0, tiled=True),
        lax.all_gather(value_local, "seq", axis=0, tiled=True),
    )
    local_rows = query_local.shape[0]
    base_start = seq_index * local_rows
    pieces = [(query_local, grad_local, base_start)]
    results = [
        attend_piece(
            rows_query,
            rows_grad,
            piece_start,
            prefix_keys,
            prefix_values,
            slab_keys,
            slab_values,
            seg_ids,
            prefix_lens,
        )
        for rows_query, rows_grad, piece_start in pieces
    ]
    key_total, value_total, prefix_ktotal, prefix_vtotal = (
        results[0][1],
        results[0][2],
        results[0][3],
        results[0][4],
    )
    query_pieces = [outcome[0].astype(jnp.bfloat16) for outcome in results]
    query_grad = query_pieces[0]
    key_mine, value_mine = (
        lax.psum_scatter(key_total, "seq", scatter_dimension=0, tiled=True),
        lax.psum_scatter(value_total, "seq", scatter_dimension=0, tiled=True),
    )
    prefix_ksum, prefix_vsum = lax.psum((prefix_ktotal, prefix_vtotal), "seq")
    prefix_key_grad = prefix_ksum.astype(jnp.bfloat16)
    prefix_value_grad = prefix_vsum.astype(jnp.bfloat16)
    query_out, key_out, value_out = (
        lax.all_to_all(query_grad, "head", split_axis=0, concat_axis=1, tiled=True),
        lax.all_to_all(
            key_mine.astype(jnp.bfloat16), "head", split_axis=0, concat_axis=1, tiled=True
        ),
        lax.all_to_all(
            value_mine.astype(jnp.bfloat16), "head", split_axis=0, concat_axis=1, tiled=True
        ),
    )
    return (query_out, key_out, value_out, prefix_key_grad, prefix_value_grad)


def solution(mesh):
    return jax.shard_map(
        on_device,
        mesh=mesh,
        in_specs=(
            P(("seq", "head"), None),
            P(("seq", "head"), None),
            P(("seq", "head"), None),
            P(("seq", "head"), None),
            P(None, "head"),
            P(None, "head"),
            P(),
            P(),
        ),
        out_specs=(
            P(("seq", "head"), None),
            P(("seq", "head"), None),
            P(("seq", "head"), None),
            P(None, "head"),
            P(None, "head"),
        ),
        check_vma=False,
    )
```

profile of v0, /device:TPU:0, one launch (start us, length us, event | category | flops | bytes accessed | tf_op | source)
XLA Modules:
  0.0 364.2 jit_solution(14358855742059171339)
XLA Ops:
  8.1 15.0 %all_to_all.124 = bf16[64,8,128]{2,0,1:T(8,128)(2,1)} all-to-all(bf16[64,8,128]{2,0,1:T(8,128)(2,1)S(1)} %copy_bitcast_fusion.5), channel_id=1, replica_groups=mesh['seq'=16,'head'=8] {'head'}, dimensions={1} | all-to-all | bytes 262144 | tf_op jit(solution)/shard_map/all_to_all | solution.py:173
  24.1 11.2 %all_to_all.125 = bf16[64,8,128]{2,0,1:T(8,128)(2,1)} all-to-all(bf16[64,8,128]{2,0,1:T(8,128)(2,1)S(1)} %copy_bitcast_fusion.4), channel_id=1, replica_groups=mesh['seq'=16,'head'=8] {'head'}, dimensions={1} | all-to-all | bytes 262144 | tf_op jit(solution)/shard_map/all_to_all | solution.py:174
  35.3 2.3 copy.111
  37.6 3.6 all-to-all-start
  42.3 17.9 %all-to-all-done = bf16[64,8,1024]{2,0,1:T(8,128)(2,1)S(1)} async-done(((bf16[64,8,1024]{2,0,1:T(8,128)(2,1)}), bf16[64,8,1024]{2,0,1:T(8,128)(2,1)S(1)}, u32[]{:S(2)}, u32[]{:S(2)}) %all-to-all-start) | async-done | bytes 1048608 | tf_op jit(solution)/shard_map/all_to_all | solution.py:171
  60.2 3.6 all-to-all-start.1
  65.1 16.8 %all-to-all-done.1 = bf16[64,8,1024]{2,0,1:T(8,128)(2,1)S(1)} async-done(((bf16[64,8,1024]{2,0,1:T(8,128)(2,1)}), bf16[64,8,1024]{2,0,1:T(8,128)(2,1)S(1)}, u32[]{:S(2)}, u32[]{:S(2)}) %all-to-all-start.1) | async-done | bytes 1048608 | tf_op jit(solution)/shard_map/all_to_all | solution.py:172
  82.9 1.5 copy.89
  86.6 1.9 copy-done.2
  88.6 3.7 %fusion.47 = (f32[8,512]{1,0:T(8,128)S(1)}, f32[8,512]{1,0:T(8,128)S(1)}, f32[256,512,8]{1,0,2:T(8,128)}) fusion(f32[256,512,8]{1,0,2:T(8,128)S(1)} %get-tuple-element.564, f32[8,512]{1,0:T(8,128)S(1)} %get-tuple-element.563, pred[512,256]{0,1:T(8,128)(4,1)S(1)} %iota_compare_fusion, bf16[512,8,128]{2,1,0:T(8,128)(2,1)S(1)} %bitcast.270, ...), kind=kOutput, calls=%fused_computation.64 | convolution fusion | flops 274718720 | bytes 9682944 | tf_op jit(solution)/shard_map/rcge,kce->cgrk/dot_general | solution.py:78
  92.2 1.7 all-gather.5.cloned.1.call-done
  94.0 18.8 %while.33 = (s32[]{:T(128)}, f32[1,8,512]{2,1,0:T(8,128)S(1)}, f32[1,8,512]{2,1,0:T(8,128)S(1)}, f32[1,8,512]{2,1,0:T(8,128)S(1)}, s32[512]{0:T(512)S(1)}, /*ind...) while((s32[]{:T(128)}, f32[1,8,512]{2,1,0:T(8,128)S(1)}, ...), condition=%wide.region_11.12_spmd.clone, body=%wide.region_4.11_spmd.clone.sunk | while | flops 1099969536 | bytes 28886388 | solution.py:106
  97.6 7.9 %conditional.6 = ((f32[1,8,512]{2,1,0:T(8,128)S(1)}, f32[1,8,512]{2,1,0:T(8,128)S(1)}, f32[1,8,512]{2,1,0:T(8,128)S(1)})) conditional(s32[]{:T(128)} %convert_element_type.72, (f32[1,8,512]{2,1,0:T(8,128)S(1)}, f32[1,8,512]{2,1,0:T(8,128)S(1)}, f32[1,8,512]{2,1,0:T(8,128)S(1)}) %tuple.96, (pred[512,512]{0,1:T(8,128)(4,1)S(1)}, ...), branch_computations={%region_6.6_spmd, %region_7.10_spmd} | conditional | flops 1098919936 | bytes 28607520 | solution.py:104
  97.6 2.5 fusion.6
  100.1 3.6 fusion.4
  103.7 1.8 fusion.5
  113.4 4.7 %fusion.54 = bf16[8,512,256]{1,2,0:T(8,128)(2,1)S(1)} fusion(f32[256,512,8]{1,0,2:T(8,128)} %get-tuple-element.565, f32[256,512,8]{1,0,2:T(8,128)} %copy-done.2, f32[8,512]{1,0:T(8,128)} %bitcast.54, f32[8,512]{1,0:T(8,128)} %bitcast.52, pred[512,256]{0,1:T(8,128)(4,1)S(1)} %iota_compare_fusion), kind=kLoop, calls=%fused_computation.73 | loop fusion | flops 6291456 | bytes 10649600 | tf_op jit(solution)/shard_map/reshape.57
  118.2 1.3 copy-done.7
  119.5 2.1 convolution_bitcast_fusion.1
  121.6 1.9 copy.68
  123.5 28.9 %while.34 = (s32[]{:T(128)}, f32[512,1,8,128]{0,3,2,1:T(8,128)S(1)}, f32[3,512,1,128]{3,1,2,0:T(8,128)}, f32[3,512,1,128]{3,1,2,0:T(8,128)}, s32[512]{0:T(512)S(...) while((s32[]{:T(128)}, ...), condition=%wide.region_16.17_spmd.clone, body=%wide.region_12.16_spmd.clone.sunk | while | flops 2706965504 | bytes 54200732 | solution.py:149
  125.9 1.7 fusion.86
  128.3 12.2 %conditional.7 = (f32[512,1,8,128]{0,3,2,1:T(8,128)S(1)}, f32[1,512,1,128]{3,1,2,0:T(8,128)S(1)}, f32[1,512,1,128]{3,1,2,0:T(8,128)S(1)}) conditional(s32[]{:T(128)} %convert_element_type.73, f32[512,1,8,128]{0,3,2,1:T(8,128)S(1)} %get-tuple-element.847, (bf16[8192,128]{1,0:T(8,128)(2,1)}, s32[]{:T(128)}, pred[512,512]{0,1:T(8,128)(4,1)}, ...), branch_computations={%region_14.14_spmd, %region_15.15_spmd} | conditional | flops 2705915904 | bytes 52872784 | solution.py:144
  128.3 2.3 fusion.34
  130.6 4.0 %fusion.22 = bf16[8,512,512]{1,2,0:T(8,128)(2,1)S(1)} fusion(f32[512,512,8]{1,0,2:T(8,128)S(1)} %fusion.34, f32[8,512]{1,0:T(8,128)} %bitcast.22, f32[8,512]{1,0:T(8,128)} %bitcast.17, pred[512,512]{0,1:T(8,128)(4,1)S(1)} %copy-done.9, bf16[512,1,8,128]{3,0,2,1:T(8,128)(2,1)S(1)} %copy-done.13, bf16[8192,128]{1,0:T(8,128)(2,1)} %get-tuple-element.283, ...), kind=kOutput, calls=%fused_computation.29 | convolution fusion | flops 549453824 | bytes 14057984 | tf_op jit(solution)/shard_map/while/body/eval_jaxpr/cond/branch_1_fun/rcge,kce->cgrk/dot_general | solution.py:112
  134.6 1.9 bitcast_add_fusion.2
  136.5 1.3 fusion.27
  137.8 2.7 fusion.28
  143.5 1.7 fusion.86
  149.0 1.7 fusion.86
  152.4 2.2 broadcast_in_dim.103.clone.1
  154.6 3.5 dynamic_update_slice.14
  158.2 2.3 broadcast_in_dim.103.clone
  160.5 3.5 dynamic_update_slice.13
  164.0 1.2 multiply_convert_fusion
  165.2 1.8 copy.71
  167.1 1.3 convert_element_type.43
  168.3 6.9 %all-to-all-start.4 = ((bf16[8,64,1024]{2,1,0:T(8,128)(2,1)}), bf16[8,64,1024]{2,1,0:T(8,128)(2,1)}, u32[]{:S(2)}, u32[]{:S(2)}) async-start(bf16[8,64,1024]{2,1,0:T(8,128)(2,1)} %convert_element_type.43), calls=%async_computation.4 | async-start | bytes 2097152 | tf_op jit(solution)/shard_map/all_to_all | solution.py:213
  175.3 3.6 %fusion.59 = f32[256,128]{1,0:T(8,128)S(1)} fusion(f32[256,512,8]{1,0,2:T(8,128)} %copy-done.2, f32[8,512]{1,0:T(8,128)} %bitcast.52, pred[512,256]{0,1:T(8,128)(4,1)S(1)} %iota_compare_fusion, bf16[512,8,128]{2,1,0:T(8,128)(2,1)S(1)} %bitcast.271), kind=kOutput, calls=%fused_computation.80 | convolution fusion | flops 272629760 | bytes 5521408 | tf_op jit(solution)/shard_map/cgrk,rcge->kce/dot_general | solution.py:126
  179.7 89.0 %reduce-scatter.5.cloned.1.call-done = f32[512,128]{1,0:T(8,128)} async-done(((f32[8192,128]{1,0:T(8,128)}), f32[512,128]{1,0:T(8,128)}) %reduce-scatter.5.cloned.1.call-update) | async-done | bytes 262160 | tf_op jit(solution)/shard_map/reduce_scatter | solution.py:207
  268.7 1.6 convert_element_type.45
  270.4 6.4 %all-to-all-start.6 = ((bf16[8,64,128]{2,1,0:T(8,128)(2,1)}), bf16[8,64,128]{2,1,0:T(8,128)(2,1)S(1)}, u32[]{:S(2)}, u32[]{:S(2)}) async-start(bf16[8,64,128]{2,1,0:T(8,128)(2,1)} %bitcast.64), calls=%async_computation.8 | async-start | bytes 262144 | tf_op jit(solution)/shard_map/all_to_all | solution.py:217
  276.8 59.3 %all-reduce.2 = (bf16[256,128]{1,0:T(8,128)(2,1)}, bf16[256,128]{1,0:T(8,128)(2,1)}) all-reduce(f32[256,128]{1,0:T(8,128)S(1)} %fusion.58, f32[256,128]{1,0:T(8,128)S(1)} %fusion.59), channel_id=1, replica_groups=mesh['seq'=16,'head'=8] {'seq'}, use_global_device_ids=true, to_apply=%region_19.20 | all-reduce | flops 65536 | bytes 393216 | tf_op jit(solution)/shard_map/psum | solution.py:209
  336.1 2.3 copy.85
  338.4 2.8 reduce-scatter.3.cloned.1.call-done
  341.2 1.6 convert_element_type.44
  342.8 6.2 %all-to-all-start.5 = ((bf16[8,64,128]{2,1,0:T(8,128)(2,1)}), bf16[8,64,128]{2,1,0:T(8,128)(2,1)S(1)}, u32[]{:S(2)}, u32[]{:S(2)}) async-start(bf16[8,64,128]{2,1,0:T(8,128)(2,1)} %bitcast.61), calls=%async_computation.6 | async-start | bytes 262144 | tf_op jit(solution)/shard_map/all_to_all | solution.py:214
  349.6 7.4 %all-to-all-done.5 = bf16[8,64,128]{2,1,0:T(8,128)(2,1)S(1)} async-done(((bf16[8,64,128]{2,1,0:T(8,128)(2,1)}), bf16[8,64,128]{2,1,0:T(8,128)(2,1)S(1)}, u32[]{:S(2)}, u32[]{:S(2)}) %all-to-all-start.5) | async-done | bytes 131104 | tf_op jit(solution)/shard_map/all_to_all | solution.py:214
  (103 shorter events, 24.5 us)
Async XLA Ops:
  7.2 0.9 copy-start
  7.2 34.0 %copy-start.11 = (bf16[64,8192]{1,0:T(8,128)(2,1)S(1)}, bf16[64,8192]{1,0:T(8,128)(2,1)}, u32[]{:S(2)}) copy-start(bf16[64,8192]{1,0:T(8,128)(2,1)} %param.19) | copy-start | bytes 3145732
  7.2 85.0 %all-gather.3.cloned.1.call-start = ((), (), s32[]{:S(2)}) async-start(), calls=%async_computation.9 | async-start | bytes 2228224 | tf_op jit(solution)/shard_map/all_gather | solution.py:177
  23.1 70.8 %all-gather.5.cloned.1.call-start = ((), (), s32[]{:S(2)}) async-start(), calls=%async_computation.10 | async-start | bytes 2228224 | tf_op jit(solution)/shard_map/all_gather | solution.py:178
  35.3 29.3 %copy-start.18 = (s32[32]{0:T(128)S(1)}, s32[32]{0:T(128)}, u32[]{:S(2)}) copy-start(s32[32]{0:T(128)} %param.23) | copy-start | bytes 388
  37.6 22.6 %all-to-all-start = ((bf16[64,8,1024]{2,0,1:T(8,128)(2,1)}), bf16[64,8,1024]{2,0,1:T(8,128)(2,1)S(1)}, u32[]{:S(2)}, u32[]{:S(2)}) async-start(bf16[64,8,1024]{2,0,1:T(8,128)(2,1)} %bitcast.264), calls=%async_computation | async-start | bytes 2097152 | tf_op jit(solution)/shard_map/all_to_all | solution.py:171
  60.2 21.7 %all-to-all-start.1 = ((bf16[64,8,1024]{2,0,1:T(8,128)(2,1)}), bf16[64,8,1024]{2,0,1:T(8,128)(2,1)S(1)}, u32[]{:S(2)}, u32[]{:S(2)}) async-start(bf16[64,8,1024]{2,0,1:T(8,128)(2,1)} %bitcast.263), calls=%async_computation.1 | async-start | bytes 2097152 | tf_op jit(solution)/shard_map/all_to_all | solution.py:172
  63.8 205.0 %reduce-scatter.5.cloned.1.call-start = ((), (), s32[]{:S(2)}) async-start(), calls=%async_computation.12 | async-start | bytes 4456448 | tf_op jit(solution)/shard_map/reduce_scatter | solution.py:207
  64.8 20.9 %copy-start.16 = (bf16[256,128]{1,0:T(8,128)(2,1)S(1)}, bf16[256,128]{1,0:T(8,128)(2,1)}, u32[]{:S(2)}) copy-start(bf16[256,128]{1,0:T(8,128)(2,1)} %param.20) | copy-start | bytes 196612
  65.1 21.6 %copy-start.5 = (bf16[64,8,8,128]{3,2,1,0:T(8,128)(2,1)}, bf16[64,8,8,128]{3,2,1,0:T(8,128)(2,1)S(1)}, u32[]{:S(2)}) copy-start(bf16[64,8,8,128]{3,2,1,0:T(8,128)(2,1)S(1)} %copy.88) | copy-start | bytes 3145732
  81.9 1.0 copy-start.10
  84.4 2.3 copy-start.3
  84.5 4.1 %copy-start.17 = (bf16[256,128]{1,0:T(8,128)(2,1)S(1)}, bf16[256,128]{1,0:T(8,128)(2,1)}, u32[]{:S(2)}) copy-start(bf16[256,128]{1,0:T(8,128)(2,1)} %param.21) | copy-start | bytes 196612
  86.6 1.9 copy-start.2
  88.6 5.4 %copy-start.12 = (bf16[512,1,8,128]{3,0,2,1:T(8,128)(2,1)S(1)}, bf16[512,1,8,128]{3,0,2,1:T(8,128)(2,1)}, u32[]{:S(2)}) copy-start(bf16[512,1,8,128]{3,0,2,1:T(8,128)(2,1)} %copy.66) | copy-start | bytes 3145732
  118.1 1.3 copy-start.7
  128.3 2.3 copy-start.9
  128.3 2.3 copy-start.13
  152.4 2.3 copy-start.15
  158.1 2.4 copy-start.14
  158.1 183.0 %reduce-scatter.3.cloned.1.call-start = ((), (), s32[]{:S(2)}) async-start(), calls=%async_computation.11 | async-start | bytes 4456448 | tf_op jit(solution)/shard_map/reduce_scatter | solution.py:206
  165.2 10.0 %copy-start.4 = (bf16[64,8,8,128]{3,2,1,0:T(8,128)(2,1)S(1)}, bf16[64,8,8,128]{3,2,1,0:T(8,128)(2,1)}, u32[]{:S(2)}) copy-start(bf16[64,8,8,128]{3,2,1,0:T(8,128)(2,1)} %copy-done.3) | copy-start | bytes 3145732
  168.3 102.0 %all-to-all-start.4 = ((bf16[8,64,1024]{2,1,0:T(8,128)(2,1)}), bf16[8,64,1024]{2,1,0:T(8,128)(2,1)}, u32[]{:S(2)}, u32[]{:S(2)}) async-start(bf16[8,64,1024]{2,1,0:T(8,128)(2,1)} %convert_element_type.43), calls=%async_computation.4 | async-start | bytes 2097152 | tf_op jit(solution)/shard_map/all_to_all | solution.py:213
  175.2 3.7 %copy-start.6 = (bf16[64,8,8,128]{3,2,1,0:T(8,128)(2,1)S(1)}, bf16[64,8,8,128]{3,2,1,0:T(8,128)(2,1)}, u32[]{:S(2)}) copy-start(bf16[64,8,8,128]{3,2,1,0:T(8,128)(2,1)} %copy-done.5) | copy-start | bytes 3145732
  175.3 3.7 %copy-start.8 = (bf16[8,512,256]{1,2,0:T(8,128)(2,1)S(1)}, bf16[8,512,256]{1,2,0:T(8,128)(2,1)}, u32[]{:S(2)}) copy-start(bf16[8,512,256]{1,2,0:T(8,128)(2,1)} %copy-done.7) | copy-start | bytes 6291460
  175.3 182.4 %copy-start.1 = (bf16[64,1024]{1,0:T(8,128)(2,1)S(1)}, bf16[64,1024]{1,0:T(8,128)(2,1)}, u32[]{:S(2)}) copy-start(bf16[64,1024]{1,0:T(8,128)(2,1)} %param.17) | copy-start | bytes 393220
  270.4 72.4 %all-to-all-start.6 = ((bf16[8,64,128]{2,1,0:T(8,128)(2,1)}), bf16[8,64,128]{2,1,0:T(8,128)(2,1)S(1)}, u32[]{:S(2)}, u32[]{:S(2)}) async-start(bf16[8,64,128]{2,1,0:T(8,128)(2,1)} %bitcast.64), calls=%async_computation.8 | async-start | bytes 262144 | tf_op jit(solution)/shard_map/all_to_all | solution.py:217
  342.8 14.2 %all-to-all-start.5 = ((bf16[8,64,128]{2,1,0:T(8,128)(2,1)}), bf16[8,64,128]{2,1,0:T(8,128)(2,1)S(1)}, u32[]{:S(2)}, u32[]{:S(2)}) async-start(bf16[8,64,128]{2,1,0:T(8,128)(2,1)} %bitcast.61), calls=%async_computation.6 | async-start | bytes 262144 | tf_op jit(solution)/shard_map/all_to_all | solution.py:214
Sparse Core Ops, SparseCore 0:
  23.3 34.0 all-gather.2
  59.1 34.8 all-gather.4
  158.3 110.4 reduce-scatter.4
  271.0 70.1 reduce-scatter.2
where the time goes:
time: 366 us; the launch traced here: 364 us
  waiting for transfers between devices  136 us (37%)
  blocking collectives  85.4 us (23%)
  local copies, waits for them, and re-layouts  44.5 us (12%)
  matrix products  29.3 us (8%)
  starting transfers between devices  26.8 us (7%)
  other arithmetic  19.9 us (5%)
  between operations  14.1 us (4%)
  loops' own time  8.55 us (2%)
    reduce_scatter x1, waiting for transfers between devices, on_device(): lax.psum_scatter(value_total, 'seq', scatter_dimension=0, tiled=True)  89 us
    psum x1, blocking collectives, on_device(): prefix_ksum, prefix_vsum = lax.psum((prefix_ktotal, prefix_vtotal), 'seq')  59.3 us
    all_to_all x1, waiting for transfers between devices, on_device(): lax.all_to_all(queries, 'head', split_axis=1, concat_axis=0, tiled=True)  17.9 us
    all_to_all x1, waiting for transfers between devices, on_device(): lax.all_to_all(out_grad, 'head', split_axis=1, concat_axis=0, tiled=True)  16.8 us
    all_to_all x1, blocking collectives, on_device(): lax.all_to_all(keys, 'head', split_axis=1, concat_axis=0, tiled=True)  15 us
    all_to_all x1, blocking collectives, on_device(): lax.all_to_all(values, 'head', split_axis=1, concat_axis=0, tiled=True)  11.2 us
    unnamed x39, local copies, waits for them, and re-layouts  10.1 us
    all_to_all x1, waiting for transfers between devices, on_device(): lax.all_to_all(key_mine.astype(jnp.bfloat16), 'head', split_axis=0, conca...  7.41 us
  transfers between devices with their start and end apart: 9, of which 6 were waited for; matrix products, arithmetic and copies ran while one was open for 9% of the time, Pallas kernels for 0%

commit v1 on v0

v1 whole, which is shorter than its diff:
```python
import math

import jax
import jax.numpy as jnp
from jax import lax
from jax.experimental import pallas as pl
from jax.experimental.pallas import tpu as pltpu
from jax.sharding import PartitionSpec as P

MESH = pl.DeviceIdType.MESH

HEAD_DIM = 128
PREFIX = 256
RING = 4
ROWS = 64
BLOCK = RING * ROWS
BACK = 4
WINDOW = (BACK + 1) * BLOCK
KEYS = PREFIX + WINDOW
OWN = PREFIX + BACK * BLOCK
SLOTS = 2
PARTS = 4
STEPS = SLOTS * PARTS
PAIR = 2 * HEAD_DIM
GROUP = 8 * HEAD_DIM
SUB = 128
NEAR = 1024 + SUB
SPAN = PREFIX + NEAR
TILE = 128
BLOCKS = 32
SEQ = 16
SEGS = 32
SCALE = HEAD_DIM**-0.5
EXP_SCALE = SCALE / math.log(2.0)
MASKED = -1e30
PIECE = PREFIX // SEQ
AHEAD = 3


def dot_nt(a, b):
    return lax.dot_general(a, b, (((1,), (1,)), ((), ())), preferred_element_type=jnp.float32)


def dot_nn(a, b):
    return lax.dot_general(a, b, (((1,), (0,)), ((), ())), preferred_element_type=jnp.float32)


def kernel(
    q,
    g,
    k,
    v,
    pk,
    pv,
    seg,
    lens,
    dq,
    dk,
    dv,
    dpk,
    dpv,
    qb,
    gb,
    kv,
    ext,
    qx,
    kt,
    acc,
    own_sum,
    s_ref,
    d_ref,
    pb_ref,
    ds_ref,
    dqb,
    part_out,
    part_in,
    own_out,
    pre_out,
    pre_in,
    pre_sum,
    kv_local,
    kv_send,
    kv_recv,
    fix_local,
    fix_send,
    fix_recv,
    win_send,
    win_recv,
    in_local,
    in_send,
    in_recv,
    dq_local,
    dq_send,
    dq_recv,
    part_send,
    part_recv,
    own_local,
    own_send,
    own_recv,
    pre_send,
    pre_recv,
    last_local,
    last_send,
    last_recv,
):
    s = lax.axis_index("seq")
    h = lax.axis_index("head")
    y = lax.rem(h, RING)
    a = h // RING
    here = 2 * s + a

    def at_y(j):
        return (s, RING * a + lax.rem(y + j, RING))

    def at_block(b):
        return (b // 2, lax.rem(b, 2) * RING + y)

    def columns(first, size):
        return pl.ds(pl.multiple_of(first, 128), size)

    def rows_of(j):
        return pl.ds(pl.multiple_of(ROWS * j, ROWS), ROWS)

    def remote(src, dst, send, recv, device):
        return pltpu.make_async_remote_copy(
            src_ref=src,
            dst_ref=dst,
            send_sem=send,
            recv_sem=recv,
            device_id=device,
            device_id_type=MESH,
        )

    barrier = pltpu.get_barrier_semaphore()
    for j in range(1, RING):
        pl.semaphore_signal(barrier, inc=1, device_id=at_y(j), device_id_type=MESH)

    def greet(d, carry):
        there = at_block(lax.rem(here + d, BLOCKS))
        pl.semaphore_signal(barrier, inc=1, device_id=there, device_id_type=MESH)
        return carry

    lax.fori_loop(1, BLOCKS, greet, 0)
    pl.semaphore_wait(barrier, RING - 1 + BLOCKS - 1)

    def kv_own(u, t):
        src = (k, v)[t].at[:, columns((RING * u + y) * HEAD_DIM, HEAD_DIM)]
        dst = kv.at[u, t, pl.ds(pl.multiple_of(OWN + ROWS * y, ROWS), ROWS)]
        return pltpu.make_async_copy(src, dst, kv_local.at[u, t])

    def kv_copy(u, t, j):
        there = lax.rem(y + j, RING)
        src = (k, v)[t].at[:, columns((RING * u + there) * HEAD_DIM, HEAD_DIM)]
        dst = kv.at[u, t, pl.ds(pl.multiple_of(OWN + ROWS * y, ROWS), ROWS)]
        return remote(src, dst, kv_send.at[u, t, j], kv_recv.at[u, t, j], at_y(j))

    def fix_own(t):
        return pltpu.make_async_copy((pk, pv)[t], kv.at[a, t, 0:PREFIX], fix_local.at[t])

    def fix_copy(t):
        device = (s, RING * (1 - a) + y)
        return remote(
            (pk, pv)[t], kv.at[a, t, 0:PREFIX], fix_send.at[t], fix_recv.at[t], device
        )

    def win_copy(u, d):
        src = kv.at[u, :, OWN:KEYS, :]
        dst = kv.at[u, :, OWN - d * BLOCK : KEYS - d * BLOCK, :]
        device = at_block(lax.rem(here + d, BLOCKS))
        return remote(src, dst, win_send.at[u, d], win_recv.at[u, d], device)

    def in_first(n, there):
        return (RING * (n // PARTS) + there) * GROUP + lax.rem(n, PARTS) * PAIR

    def in_own(n, t):
        src = (q, g)[t].at[:, columns(in_first(n, y), PAIR)]
        return pltpu.make_async_copy(src, (qb, gb)[t].at[n, rows_of(y)], in_local.at[n, t])

    def in_copy(n, t, j):
        src = (q, g)[t].at[:, columns(in_first(n, lax.rem(y + j, RING)), PAIR)]
        dst = (qb, gb)[t].at[n, rows_of(y)]
        return remote(src, dst, in_send.at[n, t, j], in_recv.at[n, t, j], at_y(j))

    def dq_own(n):
        dst = dq.at[:, columns(in_first(n, y), PAIR)]
        return pltpu.make_async_copy(dqb.at[n, rows_of(y)], dst, dq_local.at[n])

    def dq_copy(n, j):
        src = dqb.at[n, rows_of(lax.rem(y + j, RING))]
        dst = dq.at[:, columns(in_first(n, y), PAIR)]
        return remote(src, dst, dq_send.at[n, j], dq_recv.at[n, j], at_y(j))

    def part_copy(u, d):
        device = at_block(lax.rem(here + BLOCKS - d, BLOCKS))
        return remote(
            part_out.at[u, d - 1],
            part_in.at[u, d - 1],
            part_send.at[u, d],
            part_recv.at[u, d],
            device,
        )

    def own_own(u, t):
        dst = (dk, dv)[t].at[:, columns((RING * u + y) * HEAD_DIM, HEAD_DIM)]
        return pltpu.make_async_copy(own_out.at[u, t, rows_of(y)], dst, own_local.at[u, t])

    def own_copy(u, t, j):
        src = own_out.at[u, t, rows_of(lax.rem(y + j, RING))]
        dst = (dk, dv)[t].at[:, columns((RING * u + y) * HEAD_DIM, HEAD_DIM)]
        return remote(src, dst, own_send.at[u, t, j], own_recv.at[u, t, j], at_y(j))

    def piece_rows(r):
        return pl.ds(pl.multiple_of(PIECE * r, PIECE), PIECE)

    def pre_copy(u, i):
        r = lax.rem(s + i, SEQ)
        return remote(
            pre_out.at[u, :, piece_rows(r)],
            pre_in.at[here],
            pre_send.at[u, i],
            pre_recv.at[here],
            (r, RING * u + y),
        )

    def pre_wait(b):
        return remote(
            pre_out.at[0, :, 0:PIECE], pre_in.at[b], pre_send.at[0, 0], pre_recv.at[b], (s, h)
        )

    def last_own(t):
        return pltpu.make_async_copy(
            pre_sum.at[t], (dpk, dpv)[t].at[piece_rows(s)], last_local.at[t]
        )

    def last_copy(t, i):
        return remote(
            pre_sum.at[t],
            (dpk, dpv)[t].at[piece_rows(s)],
            last_send.at[t, i],
            last_recv.at[t, i],
            (lax.rem(s + i, SEQ), h),
        )

    others = range(1, RING)
    steps_back = range(1, BACK + 1)

    def send_in(n):
        for t in range(2):
            for j in (2, 1, 3):
                in_copy(n, t, j).start()
            in_own(n, t).start()

    def send_kv(u):
        for t in range(2):
            for j in (2, 1, 3):
                kv_copy(u, t, j).start()
            kv_own(u, t).start()

    def send_windows(u):
        for t in range(2):
            kv_own(u, t).wait()
            for j in others:
                kv_copy(u, t, j).wait_recv()
        for d in steps_back:
            win_copy(u, d).start()

    send_kv(0)
    for t in range(2):
        fix_copy(t).start()
        fix_own(t).start()
    send_in(0)
    send_kv(1)

    documents = lax.broadcasted_iota(jnp.int32, (128, 128), 0)
    limits = jnp.zeros((128, 128), jnp.int32)
    for e in range(SEGS):
        limits = jnp.where(documents == e, lens[e], limits)
    lanes = lax.broadcasted_iota(jnp.int32, (128, 128), 1)
    for i in range(PREFIX // 128):
        hidden = jnp.where(lanes + 128 * i < limits, 0.0, MASKED)
        ext[128 * i : 128 * (i + 1), :] = hidden.T.astype(jnp.bfloat16)
    for i in range(WINDOW // 128):
        row = 2 * here - 2 * BACK + i
        names = jnp.broadcast_to(seg[pl.ds(jnp.maximum(row, 0), 1), :], (128, 128))
        real = jnp.full((128, 128), row, jnp.int32) >= 0
        hidden = jnp.where((names == documents) & real, 0.0, MASKED)
        ext[PREFIX + 128 * i : PREFIX + 128 * (i + 1), :] = hidden.T.astype(jnp.bfloat16)
        if i >= 2 * BACK:
            picked = jnp.where(names == documents, 1.0, 0.0)
            first = 128 * (i - 2 * BACK)
            qx[first : first + 128, :] = picked.T.astype(jnp.bfloat16)

    send_windows(0)
    for n in range(1, AHEAD):
        send_in(n)

    def prepare(u):
        for d in steps_back:
            win_copy(u, d).wait_recv()
        for i in range(KEYS // 128):
            part = kv[u, 0, 128 * i : 128 * (i + 1), :].astype(jnp.float32)
            kt[:, 128 * i : 128 * (i + 1)] = part.T.astype(jnp.bfloat16)
        acc[...] = jnp.zeros_like(acc)

    def attend(n, u, i):
        first = pl.multiple_of(SUB * i, SUB)
        rows = pl.ds(first, SUB)
        near = pl.ds(pl.multiple_of(PREFIX + first, SUB), NEAR)
        q2 = jnp.concatenate([qb[n, rows, 0:HEAD_DIM], qb[n, rows, HEAD_DIM:PAIR]], axis=0)
        g2 = jnp.concatenate([gb[n, rows, 0:HEAD_DIM], gb[n, rows, HEAD_DIM:PAIR]], axis=0)
        marks = qx[rows, :]
        q_wide = jnp.concatenate([q2, jnp.concatenate([marks, marks], axis=0)], axis=1)
        s_ref[0:PREFIX, :] = dot_nt(
            jnp.concatenate([kv[u, 0, 0:PREFIX, :], ext[0:PREFIX, :]], axis=1), q_wide
        )
        s_ref[PREFIX:SPAN, :] = dot_nt(
            jnp.concatenate([kv[u, 0, near, :], ext[near, :]], axis=1), q_wide
        )
        d_ref[0:PREFIX, :] = dot_nt(kv[u, 1, 0:PREFIX, :], g2)
        d_ref[PREFIX:SPAN, :] = dot_nt(kv[u, 1, near, :], g2)
        key_at = lax.broadcasted_iota(jnp.int32, (SUB, PAIR), 0)
        row_at = lax.rem(lax.broadcasted_iota(jnp.int32, (SUB, PAIR), 1), SUB)
        s_ref[SPAN - SUB : SPAN, :] = jnp.where(
            key_at <= row_at, s_ref[SPAN - SUB : SPAN, :], MASKED
        )

        peak = jnp.full((8, PAIR), MASKED, jnp.float32)
        for f in range(0, SPAN, TILE):
            tile = s_ref[f : f + TILE, :].reshape(TILE // 8, 8, PAIR)
            peak = jnp.maximum(peak, jnp.max(tile, axis=0))
        peak = jnp.max(peak, axis=0, keepdims=True)
        total = jnp.zeros((8, PAIR), jnp.float32)
        weighted = jnp.zeros((8, PAIR), jnp.float32)
        for f in range(0, SPAN, TILE):
            weights = jnp.exp2((s_ref[f : f + TILE, :] - peak) * EXP_SCALE)
            s_ref[f : f + TILE, :] = weights
            total += jnp.sum(weights.reshape(TILE // 8, 8, PAIR), axis=0)
            dots = weights * d_ref[f : f + TILE, :]
            weighted += jnp.sum(dots.reshape(TILE // 8, 8, PAIR), axis=0)
        total = jnp.sum(total, axis=0, keepdims=True)
        weighted = jnp.sum(weighted, axis=0, keepdims=True)
        inverse = 1.0 / total
        delta = weighted * inverse
        for f in range(0, SPAN, TILE):
            probs = s_ref[f : f + TILE, :] * inverse
            pb_ref[f : f + TILE, :] = probs.astype(jnp.bfloat16)
            ds_ref[f : f + TILE, :] = (probs * (d_ref[f : f + TILE, :] - delta)).astype(
                jnp.bfloat16
            )
        acc[1, 0:PREFIX, :] += dot_nn(pb_ref[0:PREFIX, :], g2)
        acc[1, near, :] += dot_nn(pb_ref[PREFIX:SPAN, :], g2)
        acc[0, 0:PREFIX, :] += dot_nn(ds_ref[0:PREFIX, :], q2)
        acc[0, near, :] += dot_nn(ds_ref[PREFIX:SPAN, :], q2)
        grad = dot_nn(kt[:, 0:PREFIX], ds_ref[0:PREFIX, :])
        grad += dot_nn(kt[:, near], ds_ref[PREFIX:SPAN, :])
        grad = (grad * SCALE).T.astype(jnp.bfloat16)
        dqb[n, rows, 0:HEAD_DIM] = grad[0:SUB]
        dqb[n, rows, HEAD_DIM:PAIR] = grad[SUB:PAIR]

    def close(u):
        for t in range(2):
            pre_out[u, t] = acc[t, 0:PREFIX, :].astype(jnp.bfloat16)
            for d in steps_back:
                low = OWN - d * BLOCK
                part_out[u, d - 1, t] = acc[t, low : low + BLOCK, :].astype(jnp.bfloat16)
            own_sum[u, t] = acc[t, OWN:KEYS, :]
        for d in steps_back:
            part_copy(u, d).start()

        @pl.when(a == u)
        def _():
            pre_in[here] = pre_out[u, :, piece_rows(s), :]

        @pl.when(a != u)
        def _():
            pre_copy(u, 0).start()

        def spread(i, carry):
            pre_copy(u, i).start()
            return carry

        lax.fori_loop(1, SEQ, spread, 0)

    def finish(u):
        for d in steps_back:
            part_copy(u, d).wait_recv()
        for t in range(2):
            whole = own_sum[u, t]
            for d in steps_back:
                whole += part_in[u, d - 1, t].astype(jnp.float32)
            if t == 0:
                whole = whole * SCALE
            own_out[u, t] = whole.astype(jnp.bfloat16)
        for t in range(2):
            for j in (2, 1, 3):
                own_copy(u, t, j).start()
            own_own(u, t).start()

    for t in range(2):
        fix_own(t).wait()
        fix_copy(t).wait_recv()

    def step(n, carry):
        u = n // PARTS

        @pl.when(n == 1)
        def _():
            send_windows(1)

        @pl.when(n + AHEAD < STEPS)
        def _():
            send_in(n + AHEAD)

        @pl.when(lax.rem(n, PARTS) == 0)
        def _():
            prepare(u)

        for t in range(2):
            in_own(n, t).wait()
            for j in others:
                in_copy(n, t, j).wait_recv()

        def inner(i, c):
            attend(n, u, i)
            return c

        lax.fori_loop(0, BLOCK // SUB, inner, 0)
        for j in (2, 1, 3):
            dq_copy(n, j).start()
        dq_own(n).start()

        @pl.when(lax.rem(n, PARTS) == PARTS - 1)
        def _():
            close(u)

        @pl.when(n == PARTS + 1)
        def _():
            finish(0)

        return carry

    lax.fori_loop(0, STEPS, step, 0)

    def arrive(d, carry):
        pre_wait(lax.rem(here + d, BLOCKS)).wait_recv()
        return carry

    lax.fori_loop(1, BLOCKS, arrive, 0)
    for t in range(2):
        whole = jnp.sum(pre_in[:, t].astype(jnp.float32), axis=0)
        if t == 0:
            whole = whole * SCALE
        pre_sum[t] = whole.astype(jnp.bfloat16)
    for t in range(2):
        for i in range(1, SEQ):
            last_copy(t, i).start()
        last_own(t).start()
    finish(1)

    def settle(n, carry):
        for t in range(2):
            for j in others:
                in_copy(n, t, j).wait_send()
        for j in others:
            dq_copy(n, j).wait()
        dq_own(n).wait()
        return carry

    lax.fori_loop(0, STEPS, settle, 0)
    for t in range(2):
        fix_copy(t).wait_send()
        for i in range(1, SEQ):
            last_copy(t, i).wait()
        last_own(t).wait()
    for u in range(SLOTS):
        for t in range(2):
            for j in others:
                kv_copy(u, t, j).wait_send()
                own_copy(u, t, j).wait()
            own_own(u, t).wait()
        for d in steps_back:
            win_copy(u, d).wait_send()
            part_copy(u, d).wait_send()

        @pl.when(a != u)
        def _():
            pre_copy(u, 0).wait_send()

        def sent(i, carry):
            pre_copy(u, i).wait_send()
            return carry

        lax.fori_loop(1, SEQ, sent, 0)


def on_device(queries, keys, values, out_grad, prefix_keys, prefix_values, seg_ids, prefix_lens):
    bf16, f32 = jnp.bfloat16, jnp.float32
    dma = pltpu.SemaphoreType.DMA
    hbm = pl.BlockSpec(memory_space=pl.ANY)
    arrays = [
        ((STEPS, BLOCK, PAIR), bf16),
        ((STEPS, BLOCK, PAIR), bf16),
        ((SLOTS, 2, KEYS, HEAD_DIM), bf16),
        ((KEYS, 128), bf16),
        ((BLOCK, 128), bf16),
        ((HEAD_DIM, KEYS), bf16),
        ((2, KEYS, HEAD_DIM), f32),
        ((SLOTS, 2, BLOCK, HEAD_DIM), f32),
        ((SPAN, PAIR), f32),
        ((SPAN, PAIR), f32),
        ((SPAN, PAIR), bf16),
        ((SPAN, PAIR), bf16),
        ((STEPS, BLOCK, PAIR), bf16),
        ((SLOTS, BACK, 2, BLOCK, HEAD_DIM), bf16),
        ((SLOTS, BACK, 2, BLOCK, HEAD_DIM), bf16),
        ((SLOTS, 2, BLOCK, HEAD_DIM), bf16),
        ((SLOTS, 2, PREFIX, HEAD_DIM), bf16),
        ((BLOCKS, 2, PIECE, HEAD_DIM), bf16),
        ((2, PIECE, HEAD_DIM), bf16),
    ]
    semaphores = [
        (SLOTS, 2),
        (SLOTS, 2, RING),
        (SLOTS, 2, RING),
        (2,),
        (2,),
        (2,),
        (SLOTS, BACK + 1),
        (SLOTS, BACK + 1),
        (STEPS, 2),
        (STEPS, 2, RING),
        (STEPS, 2, RING),
        (STEPS,),
        (STEPS, RING),
        (STEPS, RING),
        (SLOTS, BACK + 1),
        (SLOTS, BACK + 1),
        (SLOTS, 2),
        (SLOTS, 2, RING),
        (SLOTS, 2, RING),
        (SLOTS, SEQ),
        (BLOCKS,),
        (2,),
        (2, SEQ),
        (2, SEQ),
    ]
    return pl.pallas_call(
        kernel,
        out_shape=(
            jax.ShapeDtypeStruct(queries.shape, bf16),
            jax.ShapeDtypeStruct(keys.shape, bf16),
            jax.ShapeDtypeStruct(values.shape, bf16),
            jax.ShapeDtypeStruct(prefix_keys.shape, bf16),
            jax.ShapeDtypeStruct(prefix_values.shape, bf16),
        ),
        in_specs=[hbm] * 6
        + [pl.BlockSpec(memory_space=pltpu.VMEM), pl.BlockSpec(memory_space=pltpu.SMEM)],
        out_specs=(hbm,) * 5,
        scratch_shapes=[pltpu.VMEM(shape, kind) for shape, kind in arrays]
        + [dma(shape) for shape in semaphores],
        compiler_params=pltpu.CompilerParams(
            collective_id=0, has_side_effects=True, vmem_limit_bytes=56 * 1024 * 1024
        ),
        cost_estimate=pl.CostEstimate(
            flops=4096 * SPAN * HEAD_DIM * 10,
            bytes_accessed=4 * 1024 * 1024,
            transcendentals=4096 * SPAN,
        ),
    )(
        queries,
        out_grad,
        keys,
        values,
        prefix_keys,
        prefix_values,
        seg_ids.reshape(64, 128),
        prefix_lens,
    )


def solution(mesh):
    return jax.shard_map(
        on_device,
        mesh=mesh,
        in_specs=(
            P(("seq", "head"), None),
            P(("seq", "head"), None),
            P(("seq", "head"), None),
            P(("seq", "head"), None),
            P(None, "head"),
            P(None, "head"),
            P(),
            P(),
        ),
        out_specs=(
            P(("seq", "head"), None),
            P(("seq", "head"), None),
            P(("seq", "head"), None),
            P(None, "head"),
            P(None, "head"),
        ),
        check_vma=False,
    )
```

time: 366 us -> 84.7 us (0.23)
  the two profiles are of different devices: /device:TPU:0 before, /device:TPU:5 now
where the time goes in v1:
time: 84.7 us; the launch traced here: 83.8 us
  Pallas kernels  77.6 us (92%)
  local copies, waits for them, and re-layouts  5.6 us (7%)
    pallas_call x1, Pallas kernels, on_device(): pl.pallas_call(kernel, out_shape=(jax.ShapeDtypeStruct(queries.shape, bf1...  77.6 us
    unnamed x13, local copies, waits for them, and re-layouts  5.6 us

profile of v1, /device:TPU:5, one launch (start us, length us, event | category | flops | bytes accessed | tf_op | source)
XLA Modules:
  0.0 83.8 jit_solution(7005516401092746681)
XLA Ops:
  0.6 77.6 %shard_map.119 = (bf16[64,8192]{1,0:T(8,128)(2,1)}, bf16[64,1024]{1,0:T(8,128)(2,1)}, bf16[64,1024]{1,0:T(8,128)(2,1)}, bf16[256,128]{1,0:T(8,128)(2,1)}, bf16[256,128]{1,0:T(8,128)(2,1)}) custom-call(bf16[64,8192]{1,0:T(8,128)(2,1)} %q.1, bf16[64,8192]{1,0:T(8,128)(2,1)} %g.1, bf16[64,1024]{1,0:T(8,128)(2,1)} %k.1, bf16[64,1024]{1,0:T(8,128)(2,1)} %v.1, ...), custom_call_target="tpu_custom_call" | custom-call | flops 7381975040 | bytes 4194304 | tf_op jit(solution)/shard_map/pallas_call | solution.py:547
  78.2 0.0 copy-start.1
  78.2 2.3 %copy.18 = bf16[64,8192]{1,0:T(8,128)(2,1)} copy(bf16[64,8192]{1,0:T(8,128)(2,1)} %get-tuple-element.10) | data formatting | bytes 2097152
  80.5 0.0 copy-done.1
  80.5 0.0 copy-start
  80.5 0.7 copy.19
  81.2 0.3 copy-done
  81.5 0.0 copy-start.3
  81.5 0.7 copy.20
  82.1 0.2 copy-done.3
  82.3 0.0 copy-start.2
  82.3 0.6 copy.21
  83.0 0.2 copy-done.2
  83.2 0.6 copy.22
Async XLA Ops:
  78.2 2.3 %copy-start.1 = (bf16[64,1024]{1,0:T(8,128)(2,1)S(1)}, bf16[64,1024]{1,0:T(8,128)(2,1)}, u32[]{:S(2)}) copy-start(bf16[64,1024]{1,0:T(8,128)(2,1)} %get-tuple-element.11) | copy-start | bytes 393220
  80.5 1.0 %copy-start = (bf16[64,1024]{1,0:T(8,128)(2,1)S(1)}, bf16[64,1024]{1,0:T(8,128)(2,1)}, u32[]{:S(2)}) copy-start(bf16[64,1024]{1,0:T(8,128)(2,1)} %get-tuple-element.12) | copy-start | bytes 393220
  81.5 0.9 %copy-start.3 = (bf16[256,128]{1,0:T(8,128)(2,1)S(1)}, bf16[256,128]{1,0:T(8,128)(2,1)}, u32[]{:S(2)}) copy-start(bf16[256,128]{1,0:T(8,128)(2,1)} %get-tuple-element.13) | copy-start | bytes 196612
  82.3 0.9 %copy-start.2 = (bf16[256,128]{1,0:T(8,128)(2,1)S(1)}, bf16[256,128]{1,0:T(8,128)(2,1)}, u32[]{:S(2)}) copy-start(bf16[256,128]{1,0:T(8,128)(2,1)} %get-tuple-element.14) | copy-start | bytes 196612

commit v2 on v1

--- a/solution.py
+++ b/solution.py
@@ -52,15 +52,14 @@
     v,
     pk,
     pv,
-    seg,
-    lens,
+    seg_hbm,
+    lens_hbm,
     dq,
     dk,
     dv,
     dpk,
     dpv,
-    qb,
-    gb,
+    xb,
     kv,
     ext,
     qx,
@@ -78,7 +77,9 @@
     pre_out,
     pre_in,
     pre_sum,
-    kv_local,
+    seg,
+    lens,
+    small_sem,
     kv_send,
     kv_recv,
     fix_local,
@@ -86,20 +87,16 @@
     fix_recv,
     win_send,
     win_recv,
-    in_local,
     in_send,
     in_recv,
-    dq_local,
     dq_send,
     dq_recv,
     part_send,
     part_recv,
-    own_local,
     own_send,
     own_recv,
     pre_send,
     pre_recv,
-    last_local,
     last_send,
     last_recv,
 ):
@@ -131,6 +128,16 @@
             device_id_type=MESH,
         )
 
+    small = [
+        pltpu.make_async_copy(seg_hbm, seg, small_sem.at[0]),
+        pltpu.make_async_copy(lens_hbm, lens, small_sem.at[1]),
+    ]
+    for copy in small:
+        copy.start()
+
+    def wait_for(ref, sem):
+        pltpu.make_async_copy(ref, ref, sem).wait()
+
     barrier = pltpu.get_barrier_semaphore()
     for j in range(1, RING):
         pl.semaphore_signal(barrier, inc=1, device_id=at_y(j), device_id_type=MESH)
@@ -146,68 +153,67 @@
     def kv_own(u, t):
         src = (k, v)[t].at[:, columns((RING * u + y) * HEAD_DIM, HEAD_DIM)]
         dst = kv.at[u, t, pl.ds(pl.multiple_of(OWN + ROWS * y, ROWS), ROWS)]
-        return pltpu.make_async_copy(src, dst, kv_local.at[u, t])
+        return pltpu.make_async_copy(src, dst, kv_recv.at[u])
 
     def kv_copy(u, t, j):
         there = lax.rem(y + j, RING)
         src = (k, v)[t].at[:, columns((RING * u + there) * HEAD_DIM, HEAD_DIM)]
         dst = kv.at[u, t, pl.ds(pl.multiple_of(OWN + ROWS * y, ROWS), ROWS)]
-        return remote(src, dst, kv_send.at[u, t, j], kv_recv.at[u, t, j], at_y(j))
+        return remote(src, dst, kv_send.at[0], kv_recv.at[u], at_y(j))
 
     def fix_own(t):
-        return pltpu.make_async_copy((pk, pv)[t], kv.at[a, t, 0:PREFIX], fix_local.at[t])
+        return pltpu.make_async_copy((pk, pv)[t], kv.at[a, t, 0:PREFIX], fix_local.at[0])
 
     def fix_copy(t):
         device = (s, RING * (1 - a) + y)
         return remote(
-            (pk, pv)[t], kv.at[a, t, 0:PREFIX], fix_send.at[t], fix_recv.at[t], device
+            (pk, pv)[t], kv.at[a, t, 0:PREFIX], fix_send.at[0], fix_recv.at[0], device
         )
 
     def win_copy(u, d):
         src = kv.at[u, :, OWN:KEYS, :]
         dst = kv.at[u, :, OWN - d * BLOCK : KEYS - d * BLOCK, :]
         device = at_block(lax.rem(here + d, BLOCKS))
-        return remote(src, dst, win_send.at[u, d], win_recv.at[u, d], device)
+        return remote(src, dst, win_send.at[u], win_recv.at[u], device)
 
     def in_first(n, there):
         return (RING * (n // PARTS) + there) * GROUP + lax.rem(n, PARTS) * PAIR
 
     def in_own(n, t):
         src = (q, g)[t].at[:, columns(in_first(n, y), PAIR)]
-        return pltpu.make_async_copy(src, (qb, gb)[t].at[n, rows_of(y)], in_local.at[n, t])
+        return pltpu.make_async_copy(src, xb.at[n, t, rows_of(y)], in_recv.at[n])
 
     def in_copy(n, t, j):
         src = (q, g)[t].at[:, columns(in_first(n, lax.rem(y + j, RING)), PAIR)]
-        dst = (qb, gb)[t].at[n, rows_of(y)]
-        return remote(src, dst, in_send.at[n, t, j], in_recv.at[n, t, j], at_y(j))
+        return remote(src, xb.at[n, t, rows_of(y)], in_send.at[t], in_recv.at[n], at_y(j))
 
     def dq_own(n):
         dst = dq.at[:, columns(in_first(n, y), PAIR)]
-        return pltpu.make_async_copy(dqb.at[n, rows_of(y)], dst, dq_local.at[n])
+        return pltpu.make_async_copy(dqb.at[n, rows_of(y)], dst, dq_recv.at[0])
 
     def dq_copy(n, j):
         src = dqb.at[n, rows_of(lax.rem(y + j, RING))]
         dst = dq.at[:, columns(in_first(n, y), PAIR)]
-        return remote(src, dst, dq_send.at[n, j], dq_recv.at[n, j], at_y(j))
+        return remote(src, dst, dq_send.at[0], dq_recv.at[0], at_y(j))
 
     def part_copy(u, d):
         device = at_block(lax.rem(here + BLOCKS - d, BLOCKS))
         return remote(
             part_out.at[u, d - 1],
             part_in.at[u, d - 1],
-            part_send.at[u, d],
-            part_recv.at[u, d],
+            part_send.at[u],
+            part_recv.at[u],
             device,
         )
 
     def own_own(u, t):
         dst = (dk, dv)[t].at[:, columns((RING * u + y) * HEAD_DIM, HEAD_DIM)]
-        return pltpu.make_async_copy(own_out.at[u, t, rows_of(y)], dst, own_local.at[u, t])
+        return pltpu.make_async_copy(own_out.at[u, t, rows_of(y)], dst, own_recv.at[t])
 
     def own_copy(u, t, j):
         src = own_out.at[u, t, rows_of(lax.rem(y + j, RING))]
         dst = (dk, dv)[t].at[:, columns((RING * u + y) * HEAD_DIM, HEAD_DIM)]
-        return remote(src, dst, own_send.at[u, t, j], own_recv.at[u, t, j], at_y(j))
+        return remote(src, dst, own_send.at[0], own_recv.at[t], at_y(j))
 
     def piece_rows(r):
         return pl.ds(pl.multiple_of(PIECE * r, PIECE), PIECE)
@@ -217,27 +223,22 @@
         return remote(
             pre_out.at[u, :, piece_rows(r)],
             pre_in.at[here],
-            pre_send.at[u, i],
-            pre_recv.at[here],
+            pre_send.at[0],
+            pre_recv.at[0],
             (r, RING * u + y),
-        )
-
-    def pre_wait(b):
-        return remote(
-            pre_out.at[0, :, 0:PIECE], pre_in.at[b], pre_send.at[0, 0], pre_recv.at[b], (s, h)
         )
 
     def last_own(t):
         return pltpu.make_async_copy(
-            pre_sum.at[t], (dpk, dpv)[t].at[piece_rows(s)], last_local.at[t]
+            pre_sum.at[t], (dpk, dpv)[t].at[piece_rows(s)], last_recv.at[t]
         )
 
     def last_copy(t, i):
         return remote(
             pre_sum.at[t],
             (dpk, dpv)[t].at[piece_rows(s)],
-            last_send.at[t, i],
-            last_recv.at[t, i],
+            last_send.at[0],
+            last_recv.at[t],
             (lax.rem(s + i, SEQ), h),
         )
 
@@ -257,10 +258,7 @@
             kv_own(u, t).start()
 
     def send_windows(u):
-        for t in range(2):
-            kv_own(u, t).wait()
-            for j in others:
-                kv_copy(u, t, j).wait_recv()
+        wait_for(kv.at[u, :, OWN:KEYS, :], kv_recv.at[u])
         for d in steps_back:
             win_copy(u, d).start()
 
@@ -271,6 +269,8 @@
     send_in(0)
     send_kv(1)
 
+    for copy in small:
+        copy.wait()
     documents = lax.broadcasted_iota(jnp.int32, (128, 128), 0)
     limits = jnp.zeros((128, 128), jnp.int32)
     for e in range(SEGS):
@@ -295,8 +295,7 @@
         send_in(n)
 
     def prepare(u):
-        for d in steps_back:
-            win_copy(u, d).wait_recv()
+        wait_for(kv.at[u, :, PREFIX:OWN, :], win_recv.at[u])
         for i in range(KEYS // 128):
             part = kv[u, 0, 128 * i : 128 * (i + 1), :].astype(jnp.float32)
             kt[:, 128 * i : 128 * (i + 1)] = part.T.astype(jnp.bfloat16)
@@ -306,8 +305,8 @@
         first = pl.multiple_of(SUB * i, SUB)
         rows = pl.ds(first, SUB)
         near = pl.ds(pl.multiple_of(PREFIX + first, SUB), NEAR)
-        q2 = jnp.concatenate([qb[n, rows, 0:HEAD_DIM], qb[n, rows, HEAD_DIM:PAIR]], axis=0)
-        g2 = jnp.concatenate([gb[n, rows, 0:HEAD_DIM], gb[n, rows, HEAD_DIM:PAIR]], axis=0)
+        q2 = jnp.concatenate([xb[n, 0, rows, 0:HEAD_DIM], xb[n, 0, rows, HEAD_DIM:PAIR]], axis=0)
+        g2 = jnp.concatenate([xb[n, 1, rows, 0:HEAD_DIM], xb[n, 1, rows, HEAD_DIM:PAIR]], axis=0)
         marks = qx[rows, :]
         q_wide = jnp.concatenate([q2, jnp.concatenate([marks, marks], axis=0)], axis=1)
         s_ref[0:PREFIX, :] = dot_nt(
@@ -382,8 +381,7 @@
         lax.fori_loop(1, SEQ, spread, 0)
 
     def finish(u):
-        for d in steps_back:
-            part_copy(u, d).wait_recv()
+        wait_for(part_in.at[u], part_recv.at[u])
         for t in range(2):
             whole = own_sum[u, t]
             for d in steps_back:
@@ -396,9 +394,8 @@
                 own_copy(u, t, j).start()
             own_own(u, t).start()
 
-    for t in range(2):
-        fix_own(t).wait()
-        fix_copy(t).wait_recv()
+    wait_for(kv.at[0, :, 0:PREFIX], fix_local.at[0])
+    wait_for(kv.at[0, :, 0:PREFIX], fix_recv.at[0])
 
     def step(n, carry):
         u = n // PARTS
@@ -415,10 +412,7 @@
         def _():
             prepare(u)
 
-        for t in range(2):
-            in_own(n, t).wait()
-            for j in others:
-                in_copy(n, t, j).wait_recv()
+        wait_for(xb.at[n], in_recv.at[n])
 
         def inner(i, c):
             attend(n, u, i)
@@ -441,11 +435,7 @@
 
     lax.fori_loop(0, STEPS, step, 0)
 
-    def arrive(d, carry):
-        pre_wait(lax.rem(here + d, BLOCKS)).wait_recv()
-        return carry
-
-    lax.fori_loop(1, BLOCKS, arrive, 0)
+    wait_for(pre_in.at[0 : BLOCKS - 1], pre_recv.at[0])
     for t in range(2):
         whole = jnp.sum(pre_in[:, t].astype(jnp.float32), axis=0)
         if t == 0:
@@ -457,40 +447,46 @@
         last_own(t).start()
     finish(1)
 
-    def settle(n, carry):
-        for t in range(2):
-            for j in others:
-                in_copy(n, t, j).wait_send()
-        for j in others:
-            dq_copy(n, j).wait()
-        dq_own(n).wait()
-        return carry
-
-    lax.fori_loop(0, STEPS, settle, 0)
     for t in range(2):
-        fix_copy(t).wait_send()
-        for i in range(1, SEQ):
-            last_copy(t, i).wait()
-        last_own(t).wait()
+        wait_for(xb.at[0:6, t], in_send.at[t])
+        wait_for((dk, dv)[t], own_recv.at[t])
+        wait_for((dpk, dpv)[t], last_recv.at[t])
+    wait_for(dqb.at[0:6], dq_send.at[0])
+    wait_for(dq, dq_recv.at[0])
+    wait_for(own_out.at[:, :, 0 : BLOCK - ROWS], kv_send.at[0])
+    wait_for(own_out.at[:, :, 0 : BLOCK - ROWS], own_send.at[0])
+    wait_for(pre_out.at[0], fix_send.at[0])
+    wait_for(pre_out.at[0, :, 0 : PREFIX - PIECE], last_send.at[0])
+    wait_for(pre_in.at[0 : BLOCKS - 1], pre_send.at[0])
     for u in range(SLOTS):
-        for t in range(2):
-            for j in others:
-                kv_copy(u, t, j).wait_send()
-                own_copy(u, t, j).wait()
-            own_own(u, t).wait()
-        for d in steps_back:
-            win_copy(u, d).wait_send()
-            part_copy(u, d).wait_send()
-
-        @pl.when(a != u)
-        def _():
-            pre_copy(u, 0).wait_send()
-
-        def sent(i, carry):
-            pre_copy(u, i).wait_send()
-            return carry
-
-        lax.fori_loop(1, SEQ, sent, 0)
+        wait_for(kv.at[u, :, PREFIX:OWN, :], win_send.at[u])
+        wait_for(part_out.at[u], part_send.at[u])
+
+
+def hand_over(*refs):
+    count = (len(refs) - 2) // 3
+    before, after, held = refs[:count], refs[count : 2 * count], refs[2 * count : 3 * count]
+    arrived, stored = refs[-2:]
+    pieces = []
+    for i in range(count):
+        rows = before[i].shape[0]
+        size = 16 if before[i].shape[1] > GROUP else rows
+        for first in range(0, rows, size):
+            n = len(pieces)
+            part = pl.ds(first, size)
+            pieces.append(
+                (
+                    pltpu.make_async_copy(before[i].at[part], held[i].at[part], arrived.at[n]),
+                    pltpu.make_async_copy(held[i].at[part], after[i].at[part], stored.at[n]),
+                )
+            )
+    for load, store in pieces:
+        load.start()
+    for load, store in pieces:
+        load.wait()
+        store.start()
+    for load, store in pieces:
+        store.wait()
 
 
 def on_device(queries, keys, values, out_grad, prefix_keys, prefix_values, seg_ids, prefix_lens):
@@ -498,8 +494,7 @@
     dma = pltpu.SemaphoreType.DMA
     hbm = pl.BlockSpec(memory_space=pl.ANY)
     arrays = [
-        ((STEPS, BLOCK, PAIR), bf16),
-        ((STEPS, BLOCK, PAIR), bf16),
+        ((STEPS, 2, BLOCK, PAIR), bf16),
         ((SLOTS, 2, KEYS, HEAD_DIM), bf16),
         ((KEYS, 128), bf16),
         ((BLOCK, 128), bf16),
@@ -519,45 +514,42 @@
         ((2, PIECE, HEAD_DIM), bf16),
     ]
     semaphores = [
-        (SLOTS, 2),
-        (SLOTS, 2, RING),
-        (SLOTS, 2, RING),
-        (2,),
-        (2,),
-        (2,),
-        (SLOTS, BACK + 1),
-        (SLOTS, BACK + 1),
-        (STEPS, 2),
-        (STEPS, 2, RING),
-        (STEPS, 2, RING),
-        (STEPS,),
-        (STEPS, RING),
-        (STEPS, RING),
-        (SLOTS, BACK + 1),
-        (SLOTS, BACK + 1),
-        (SLOTS, 2),
-        (SLOTS, 2, RING),
-        (SLOTS, 2, RING),
-        (SLOTS, SEQ),
-        (BLOCKS,),
-        (2,),
-        (2, SEQ),
-        (2, SEQ),
+        2,
+        1,
+        SLOTS,
+        1,
+        1,
+        1,
+        SLOTS,
+        SLOTS,
+        2,
+        STEPS,
+        1,
+        1,
+        SLOTS,
+        SLOTS,
+        1,
+        2,
+        1,
+        1,
+        1,
+        2,
     ]
-    return pl.pallas_call(
+    results = (
+        jax.ShapeDtypeStruct(queries.shape, bf16),
+        jax.ShapeDtypeStruct(keys.shape, bf16),
+        jax.ShapeDtypeStruct(values.shape, bf16),
+        jax.ShapeDtypeStruct(prefix_keys.shape, bf16),
+        jax.ShapeDtypeStruct(prefix_values.shape, bf16),
+    )
+    raw = pl.pallas_call(
         kernel,
-        out_shape=(
-            jax.ShapeDtypeStruct(queries.shape, bf16),
-            jax.ShapeDtypeStruct(keys.shape, bf16),
-            jax.ShapeDtypeStruct(values.shape, bf16),
-            jax.ShapeDtypeStruct(prefix_keys.shape, bf16),
-            jax.ShapeDtypeStruct(prefix_values.shape, bf16),
-        ),
-        in_specs=[hbm] * 6
-        + [pl.BlockSpec(memory_space=pltpu.VMEM), pl.BlockSpec(memory_space=pltpu.SMEM)],
+        out_shape=results,
+        in_specs=[hbm] * 8,
         out_specs=(hbm,) * 5,
         scratch_shapes=[pltpu.VMEM(shape, kind) for shape, kind in arrays]
-        + [dma(shape) for shape in semaphores],
+        + [pltpu.VMEM((64, 128), jnp.int32), pltpu.SMEM((SEGS,), jnp.int32)]
+        + [dma((size,)) for size in semaphores],
         compiler_params=pltpu.CompilerParams(
             collective_id=0, has_side_effects=True, vmem_limit_bytes=56 * 1024 * 1024
         ),
@@ -576,6 +568,13 @@
         seg_ids.reshape(64, 128),
         prefix_lens,
     )
+    return pl.pallas_call(
+        hand_over,
+        out_shape=results,
+        in_specs=[hbm] * len(results),
+        out_specs=(hbm,) * len(results),
+        scratch_shapes=[pltpu.VMEM(x.shape, x.dtype) for x in results] + [dma((16,)), dma((16,))],
+    )(*raw)
 
 
 def solution(mesh):

time: 84.7 us -> 76.1 us (0.90)
  local copies, waits for them, and re-layouts: 5.6 us -> 0 us
  Pallas kernels: 77.6 us -> 74.8 us
    unnamed x13 -> x0, local copies, waits for them, and re-layouts: 5.6 us -> none
    pallas_call x1 -> x2, Pallas kernels: 77.6 us -> 74.8 us  [the longest x1 72.5 us: on_device(): pl.pallas_call(kernel, out_shape=results, in_specs=[hbm] * 8, out_specs=(...]
where the time goes in v2:
time: 76.1 us; the launch traced here: 75.4 us
  Pallas kernels  74.8 us (98%)
    pallas_call x1, Pallas kernels, on_device(): pl.pallas_call(kernel, out_shape=results, in_specs=[hbm] * 8, out_specs=(...  72.5 us
    pallas_call x1, Pallas kernels, on_device(): pl.pallas_call(hand_over, out_shape=results, in_specs=[hbm] * len(results...  2.32 us

profile of v2, /device:TPU:5, one launch (start us, length us, event | category | flops | bytes accessed | tf_op | source)
XLA Modules:
  0.0 75.4 jit_solution(17514906226114654478)
XLA Ops:
  0.6 72.5 %shard_map.119 = (bf16[64,8192]{1,0:T(8,128)(2,1)}, bf16[64,1024]{1,0:T(8,128)(2,1)}, bf16[64,1024]{1,0:T(8,128)(2,1)}, bf16[256,128]{1,0:T(8,128)(2,1)}, bf16[256,128]{1,0:T(8,128)(2,1)}) custom-call(bf16[64,8192]{1,0:T(8,128)(2,1)} %q.1, bf16[64,8192]{1,0:T(8,128)(2,1)} %g.1, bf16[64,1024]{1,0:T(8,128)(2,1)} %k.1, bf16[64,1024]{1,0:T(8,128)(2,1)} %v.1, ...), custom_call_target="tpu_custom_call" | custom-call | flops 7381975040 | bytes 4194304 | tf_op jit(solution)/shard_map/pallas_call | solution.py:545
  73.1 2.3 %shard_map.120 = (bf16[64,8192]{1,0:T(8,128)(2,1)}, bf16[64,1024]{1,0:T(8,128)(2,1)}, bf16[64,1024]{1,0:T(8,128)(2,1)}, bf16[256,128]{1,0:T(8,128)(2,1)}, bf16[256,128]{1,0:T(8,128)(2,1)}) custom-call(bf16[64,8192]{1,0:T(8,128)(2,1)} %get-tuple-element.10.refs_0_, bf16[64,1024]{1,0:T(8,128)(2,1)} %get-tuple-element.11.refs_1_, ...), custom_call_target="tpu_custom_call" | custom-call | tf_op jit(solution)/shard_map/pallas_call | solution.py:571

commit v3 on v2

--- a/solution.py
+++ b/solution.py
@@ -19,14 +19,17 @@
 KEYS = PREFIX + WINDOW
 OWN = PREFIX + BACK * BLOCK
 SLOTS = 2
-PARTS = 4
+HEADS = 4
+PARTS = 2
 STEPS = SLOTS * PARTS
-PAIR = 2 * HEAD_DIM
-GROUP = 8 * HEAD_DIM
+WIDE = HEADS * HEAD_DIM
+GROUP = PARTS * WIDE
 SUB = 128
 NEAR = 1024 + SUB
 SPAN = PREFIX + NEAR
 TILE = 128
+HALF = 256
+CUTS = [(0, PREFIX)] + [(PREFIX + NEAR // 3 * i, NEAR // 3) for i in range(3)]
 BLOCKS = 32
 SEQ = 16
 SEGS = 32
@@ -34,7 +37,6 @@
 EXP_SCALE = SCALE / math.log(2.0)
 MASKED = -1e30
 PIECE = PREFIX // SEQ
-AHEAD = 3
 
 
 def dot_nt(a, b):
@@ -66,10 +68,14 @@
     kt,
     acc,
     own_sum,
-    s_ref,
-    d_ref,
-    pb_ref,
-    ds_ref,
+    s_0,
+    d_0,
+    p_0,
+    ds_0,
+    s_1,
+    d_1,
+    p_1,
+    ds_1,
     dqb,
     part_out,
     part_in,
@@ -148,8 +154,6 @@
         return carry
 
     lax.fori_loop(1, BLOCKS, greet, 0)
-    pl.semaphore_wait(barrier, RING - 1 + BLOCKS - 1)
-
     def kv_own(u, t):
         src = (k, v)[t].at[:, columns((RING * u + y) * HEAD_DIM, HEAD_DIM)]
         dst = kv.at[u, t, pl.ds(pl.multiple_of(OWN + ROWS * y, ROWS), ROWS)]
@@ -177,32 +181,32 @@
         return remote(src, dst, win_send.at[u], win_recv.at[u], device)
 
     def in_first(n, there):
-        return (RING * (n // PARTS) + there) * GROUP + lax.rem(n, PARTS) * PAIR
+        return (RING * (n // PARTS) + there) * GROUP + lax.rem(n, PARTS) * WIDE
 
     def in_own(n, t):
-        src = (q, g)[t].at[:, columns(in_first(n, y), PAIR)]
+        src = (q, g)[t].at[:, columns(in_first(n, y), WIDE)]
         return pltpu.make_async_copy(src, xb.at[n, t, rows_of(y)], in_recv.at[n])
 
     def in_copy(n, t, j):
-        src = (q, g)[t].at[:, columns(in_first(n, lax.rem(y + j, RING)), PAIR)]
+        src = (q, g)[t].at[:, columns(in_first(n, lax.rem(y + j, RING)), WIDE)]
         return remote(src, xb.at[n, t, rows_of(y)], in_send.at[t], in_recv.at[n], at_y(j))
 
     def dq_own(n):
-        dst = dq.at[:, columns(in_first(n, y), PAIR)]
+        dst = dq.at[:, columns(in_first(n, y), WIDE)]
         return pltpu.make_async_copy(dqb.at[n, rows_of(y)], dst, dq_recv.at[0])
 
     def dq_copy(n, j):
         src = dqb.at[n, rows_of(lax.rem(y + j, RING))]
-        dst = dq.at[:, columns(in_first(n, y), PAIR)]
+        dst = dq.at[:, columns(in_first(n, y), WIDE)]
         return remote(src, dst, dq_send.at[0], dq_recv.at[0], at_y(j))
 
-    def part_copy(u, d):
+    def part_copy(u, t, d):
         device = at_block(lax.rem(here + BLOCKS - d, BLOCKS))
         return remote(
-            part_out.at[u, d - 1],
-            part_in.at[u, d - 1],
-            part_send.at[u],
-            part_recv.at[u],
+            part_out.at[u, t, d - 1],
+            part_in.at[u, t, d - 1],
+            part_send.at[u, t],
+            part_recv.at[u, t],
             device,
         )
 
@@ -249,25 +253,24 @@
         for t in range(2):
             for j in (2, 1, 3):
                 in_copy(n, t, j).start()
-            in_own(n, t).start()
 
     def send_kv(u):
         for t in range(2):
             for j in (2, 1, 3):
                 kv_copy(u, t, j).start()
-            kv_own(u, t).start()
 
     def send_windows(u):
         wait_for(kv.at[u, :, OWN:KEYS, :], kv_recv.at[u])
         for d in steps_back:
             win_copy(u, d).start()
 
-    send_kv(0)
     for t in range(2):
-        fix_copy(t).start()
+        for u in range(SLOTS):
+            kv_own(u, t).start()
         fix_own(t).start()
-    send_in(0)
-    send_kv(1)
+    for n in range(STEPS):
+        for t in range(2):
+            in_own(n, t).start()
 
     for copy in small:
         copy.wait()
@@ -290,8 +293,15 @@
             first = 128 * (i - 2 * BACK)
             qx[first : first + 128, :] = picked.T.astype(jnp.bfloat16)
 
+    pl.semaphore_wait(barrier, RING - 1 + BLOCKS - 1)
+    send_kv(0)
+    for t in range(2):
+        fix_copy(t).start()
+    send_in(0)
+    send_kv(1)
+
     send_windows(0)
-    for n in range(1, AHEAD):
+    for n in range(1, STEPS):
         send_in(n)
 
     def prepare(u):
@@ -301,70 +311,152 @@
             kt[:, 128 * i : 128 * (i + 1)] = part.T.astype(jnp.bfloat16)
         acc[...] = jnp.zeros_like(acc)
 
-    def attend(n, u, i):
-        first = pl.multiple_of(SUB * i, SUB)
-        rows = pl.ds(first, SUB)
-        near = pl.ds(pl.multiple_of(PREFIX + first, SUB), NEAR)
-        q2 = jnp.concatenate([xb[n, 0, rows, 0:HEAD_DIM], xb[n, 0, rows, HEAD_DIM:PAIR]], axis=0)
-        g2 = jnp.concatenate([xb[n, 1, rows, 0:HEAD_DIM], xb[n, 1, rows, HEAD_DIM:PAIR]], axis=0)
-        marks = qx[rows, :]
-        q_wide = jnp.concatenate([q2, jnp.concatenate([marks, marks], axis=0)], axis=1)
-        s_ref[0:PREFIX, :] = dot_nt(
-            jnp.concatenate([kv[u, 0, 0:PREFIX, :], ext[0:PREFIX, :]], axis=1), q_wide
+    passes = ((s_0, d_0, p_0, ds_0), (s_1, d_1, p_1, ds_1))
+
+    def key_rows(i, cut):
+        first, size = cut
+        return pl.ds(first if first < PREFIX else first + SUB * i, size)
+
+    def load_rows(n, t, i):
+        rows = pl.ds(SUB * i, SUB)
+        return jnp.concatenate(
+            [xb[n, t, rows, HEAD_DIM * x : HEAD_DIM * (x + 1)] for x in range(HEADS)], axis=0
         )
-        s_ref[PREFIX:SPAN, :] = dot_nt(
-            jnp.concatenate([kv[u, 0, near, :], ext[near, :]], axis=1), q_wide
-        )
-        d_ref[0:PREFIX, :] = dot_nt(kv[u, 1, 0:PREFIX, :], g2)
-        d_ref[PREFIX:SPAN, :] = dot_nt(kv[u, 1, near, :], g2)
-        key_at = lax.broadcasted_iota(jnp.int32, (SUB, PAIR), 0)
-        row_at = lax.rem(lax.broadcasted_iota(jnp.int32, (SUB, PAIR), 1), SUB)
-        s_ref[SPAN - SUB : SPAN, :] = jnp.where(
-            key_at <= row_at, s_ref[SPAN - SUB : SPAN, :], MASKED
-        )
-
-        peak = jnp.full((8, PAIR), MASKED, jnp.float32)
-        for f in range(0, SPAN, TILE):
-            tile = s_ref[f : f + TILE, :].reshape(TILE // 8, 8, PAIR)
-            peak = jnp.maximum(peak, jnp.max(tile, axis=0))
-        peak = jnp.max(peak, axis=0, keepdims=True)
-        total = jnp.zeros((8, PAIR), jnp.float32)
-        weighted = jnp.zeros((8, PAIR), jnp.float32)
-        for f in range(0, SPAN, TILE):
-            weights = jnp.exp2((s_ref[f : f + TILE, :] - peak) * EXP_SCALE)
-            s_ref[f : f + TILE, :] = weights
-            total += jnp.sum(weights.reshape(TILE // 8, 8, PAIR), axis=0)
-            dots = weights * d_ref[f : f + TILE, :]
-            weighted += jnp.sum(dots.reshape(TILE // 8, 8, PAIR), axis=0)
-        total = jnp.sum(total, axis=0, keepdims=True)
-        weighted = jnp.sum(weighted, axis=0, keepdims=True)
-        inverse = 1.0 / total
-        delta = weighted * inverse
-        for f in range(0, SPAN, TILE):
-            probs = s_ref[f : f + TILE, :] * inverse
-            pb_ref[f : f + TILE, :] = probs.astype(jnp.bfloat16)
-            ds_ref[f : f + TILE, :] = (probs * (d_ref[f : f + TILE, :] - delta)).astype(
-                jnp.bfloat16
-            )
-        acc[1, 0:PREFIX, :] += dot_nn(pb_ref[0:PREFIX, :], g2)
-        acc[1, near, :] += dot_nn(pb_ref[PREFIX:SPAN, :], g2)
-        acc[0, 0:PREFIX, :] += dot_nn(ds_ref[0:PREFIX, :], q2)
-        acc[0, near, :] += dot_nn(ds_ref[PREFIX:SPAN, :], q2)
-        grad = dot_nn(kt[:, 0:PREFIX], ds_ref[0:PREFIX, :])
-        grad += dot_nn(kt[:, near], ds_ref[PREFIX:SPAN, :])
-        grad = (grad * SCALE).T.astype(jnp.bfloat16)
-        dqb[n, rows, 0:HEAD_DIM] = grad[0:SUB]
-        dqb[n, rows, HEAD_DIM:PAIR] = grad[SUB:PAIR]
+
+    def score(u, i, q2, g2):
+        s_ref, d_ref, _, _ = passes[i]
+        marks = jnp.concatenate([qx[pl.ds(SUB * i, SUB), :]] * HEADS, axis=0)
+        q_wide = jnp.concatenate([q2, marks], axis=1)
+
+        def keys(cut):
+            rows = key_rows(i, cut)
+            wide = jnp.concatenate([kv[u, 0, rows, :], ext[rows, :]], axis=1)
+            s_ref[pl.ds(*cut), :] = dot_nt(wide, q_wide)
+
+        def values(cut):
+            d_ref[pl.ds(*cut), :] = dot_nt(kv[u, 1, key_rows(i, cut), :], g2)
+
+        for cut in CUTS:
+            yield lambda: keys(cut)
+        for cut in CUTS:
+            yield lambda: values(cut)
+
+    def weigh(i, first):
+        s_ref, d_ref, p_ref, ds_ref = passes[i]
+        tiles = [pl.ds(f, TILE) for f in range(0, SPAN, TILE)]
+        key_at = lax.broadcasted_iota(jnp.int32, (SUB, HALF), 0)
+        row_at = lax.rem(lax.broadcasted_iota(jnp.int32, (SUB, HALF), 1), SUB)
+
+        def fold(tile):
+            return tile.reshape(TILE // 8, 8, HALF)
+
+        for c in range(0, WIDE, HALF):
+            cols = pl.ds(c, HALF)
+            out = pl.ds(pl.multiple_of(first + c, HALF), HALF)
+            has = {}
+
+            def begin():
+                last = pl.ds(SPAN - SUB, SUB)
+                s_ref[last, cols] = jnp.where(key_at <= row_at, s_ref[last, cols], MASKED)
+                has["peak"] = jnp.full((8, HALF), MASKED, jnp.float32)
+                has["total"] = jnp.zeros((8, HALF), jnp.float32)
+                has["weighted"] = jnp.zeros((8, HALF), jnp.float32)
+
+            def top(tile):
+                has["peak"] = jnp.maximum(has["peak"], jnp.max(fold(s_ref[tile, cols]), axis=0))
+
+            def level():
+                has["peak"] = jnp.max(has["peak"], axis=0, keepdims=True)
+
+            def weight(tile):
+                weights = jnp.exp2((s_ref[tile, cols] - has["peak"]) * EXP_SCALE)
+                s_ref[tile, cols] = weights
+                has["total"] += jnp.sum(fold(weights), axis=0)
+                has["weighted"] += jnp.sum(fold(weights * d_ref[tile, cols]), axis=0)
+
+            def settle():
+                has["inverse"] = 1.0 / jnp.sum(has["total"], axis=0, keepdims=True)
+                weighted = jnp.sum(has["weighted"], axis=0, keepdims=True)
+                has["delta"] = weighted * has["inverse"]
+
+            def grade(tile):
+                probs = s_ref[tile, cols] * has["inverse"]
+                p_ref[tile, cols] = probs.astype(jnp.bfloat16)
+                score_grad = probs * (d_ref[tile, cols] - has["delta"])
+                ds_ref[tile, out] = score_grad.astype(jnp.bfloat16)
+
+            yield begin
+            for tile in tiles:
+                yield lambda: top(tile)
+            yield level
+            for tile in tiles:
+                yield lambda: weight(tile)
+            yield settle
+            for tile in tiles:
+                yield lambda: grade(tile)
+
+    def gather_up(i, first, q2, g2):
+        _, _, p_ref, ds_ref = passes[i]
+        cols = pl.ds(pl.multiple_of(first, WIDE), WIDE)
+
+        def values(cut):
+            acc[1, key_rows(i, cut), :] += dot_nn(p_ref[pl.ds(*cut), :], g2)
+
+        def keys(cut):
+            acc[0, key_rows(i, cut), :] += dot_nn(ds_ref[pl.ds(*cut), cols], q2)
+
+        for cut in CUTS:
+            yield lambda: values(cut)
+        for cut in CUTS:
+            yield lambda: keys(cut)
+
+    def together(products, count, others, other_count):
+        done = 0
+        for i in range(other_count):
+            while done < count and done * other_count <= i * count:
+                next(products)()
+                done += 1
+            next(others)()
+        for rest in products:
+            rest()
+
+    def attend(n, u):
+        first = lax.rem(n, PARTS) * WIDE
+        held = [[load_rows(n, t, i) for t in range(2)] for i in range(2)]
+        products = 2 * len(CUTS)
+        passing = WIDE // HALF * (3 * (SPAN // TILE) + 3)
+        for do in score(u, 0, *held[0]):
+            do()
+        together(score(u, 1, *held[1]), products, weigh(0, first), passing)
+        together(gather_up(0, first, *held[0]), products, weigh(1, first), passing)
+        for do in gather_up(1, first, *held[1]):
+            do()
+
+    def query_part(u):
+        for i in range(2):
+            _, _, _, ds_ref = passes[i]
+            rows = pl.ds(SUB * i, SUB)
+            near = pl.ds(PREFIX + SUB * i, NEAR)
+            grad = dot_nn(kt[:, 0:PREFIX], ds_ref[0:PREFIX, :])
+            grad += dot_nn(kt[:, near], ds_ref[PREFIX:SPAN, :])
+            grad = (grad * SCALE).T.astype(jnp.bfloat16)
+            for x in range(PARTS * HEADS):
+                cols = pl.ds(HEAD_DIM * (x % HEADS), HEAD_DIM)
+                dqb[PARTS * u + x // HEADS, rows, cols] = grad[SUB * x : SUB * (x + 1)]
+        for n in range(PARTS):
+            for j in (2, 1, 3):
+                dq_copy(PARTS * u + n, j).start()
+            dq_own(PARTS * u + n).start()
 
     def close(u):
+        for t in (1, 0):
+            for d in steps_back:
+                low = OWN - d * BLOCK
+                part_out[u, t, d - 1] = acc[t, low : low + BLOCK, :].astype(jnp.bfloat16)
+                part_copy(u, t, d).start()
         for t in range(2):
             pre_out[u, t] = acc[t, 0:PREFIX, :].astype(jnp.bfloat16)
-            for d in steps_back:
-                low = OWN - d * BLOCK
-                part_out[u, d - 1, t] = acc[t, low : low + BLOCK, :].astype(jnp.bfloat16)
             own_sum[u, t] = acc[t, OWN:KEYS, :]
-        for d in steps_back:
-            part_copy(u, d).start()
 
         @pl.when(a == u)
         def _():
@@ -381,77 +473,76 @@
         lax.fori_loop(1, SEQ, spread, 0)
 
     def finish(u):
-        wait_for(part_in.at[u], part_recv.at[u])
-        for t in range(2):
+        for t in (1, 0):
+            wait_for(part_in.at[u, t], part_recv.at[u, t])
             whole = own_sum[u, t]
             for d in steps_back:
-                whole += part_in[u, d - 1, t].astype(jnp.float32)
+                whole += part_in[u, t, d - 1].astype(jnp.float32)
             if t == 0:
                 whole = whole * SCALE
             own_out[u, t] = whole.astype(jnp.bfloat16)
-        for t in range(2):
             for j in (2, 1, 3):
                 own_copy(u, t, j).start()
             own_own(u, t).start()
 
+    def hand_prefix(u):
+        @pl.when(a == u)
+        def _():
+            wait_for(pre_in.at[0 : BLOCKS - 1], pre_recv.at[0])
+            for t in range(2):
+                whole = jnp.sum(pre_in[:, t].astype(jnp.float32), axis=0)
+                if t == 0:
+                    whole = whole * SCALE
+                pre_sum[t] = whole.astype(jnp.bfloat16)
+            for t in range(2):
+                for i in range(1, SEQ):
+                    last_copy(t, i).start()
+                last_own(t).start()
+
     wait_for(kv.at[0, :, 0:PREFIX], fix_local.at[0])
     wait_for(kv.at[0, :, 0:PREFIX], fix_recv.at[0])
 
     def step(n, carry):
         u = n // PARTS
 
-        @pl.when(n == 1)
+        @pl.when(n == 0)
         def _():
             send_windows(1)
 
-        @pl.when(n + AHEAD < STEPS)
-        def _():
-            send_in(n + AHEAD)
-
         @pl.when(lax.rem(n, PARTS) == 0)
         def _():
             prepare(u)
 
         wait_for(xb.at[n], in_recv.at[n])
 
-        def inner(i, c):
-            attend(n, u, i)
-            return c
-
-        lax.fori_loop(0, BLOCK // SUB, inner, 0)
-        for j in (2, 1, 3):
-            dq_copy(n, j).start()
-        dq_own(n).start()
+        attend(n, u)
 
         @pl.when(lax.rem(n, PARTS) == PARTS - 1)
         def _():
             close(u)
 
-        @pl.when(n == PARTS + 1)
+        @pl.when(n == PARTS - 1)
+        def _():
+            query_part(0)
+
+        @pl.when(n == PARTS)
         def _():
             finish(0)
+            hand_prefix(0)
 
         return carry
 
     lax.fori_loop(0, STEPS, step, 0)
 
-    wait_for(pre_in.at[0 : BLOCKS - 1], pre_recv.at[0])
+    query_part(1)
+    hand_prefix(1)
+    finish(1)
+
     for t in range(2):
-        whole = jnp.sum(pre_in[:, t].astype(jnp.float32), axis=0)
-        if t == 0:
-            whole = whole * SCALE
-        pre_sum[t] = whole.astype(jnp.bfloat16)
-    for t in range(2):
-        for i in range(1, SEQ):
-            last_copy(t, i).start()
-        last_own(t).start()
-    finish(1)
-
-    for t in range(2):
-        wait_for(xb.at[0:6, t], in_send.at[t])
+        wait_for(xb.at[0:3, t], in_send.at[t])
         wait_for((dk, dv)[t], own_recv.at[t])
         wait_for((dpk, dpv)[t], last_recv.at[t])
-    wait_for(dqb.at[0:6], dq_send.at[0])
+    wait_for(dqb.at[0:3], dq_send.at[0])
     wait_for(dq, dq_recv.at[0])
     wait_for(own_out.at[:, :, 0 : BLOCK - ROWS], kv_send.at[0])
     wait_for(own_out.at[:, :, 0 : BLOCK - ROWS], own_send.at[0])
@@ -460,7 +551,8 @@
     wait_for(pre_in.at[0 : BLOCKS - 1], pre_send.at[0])
     for u in range(SLOTS):
         wait_for(kv.at[u, :, PREFIX:OWN, :], win_send.at[u])
-        wait_for(part_out.at[u], part_send.at[u])
+        for t in range(2):
+            wait_for(part_out.at[u, t], part_send.at[u, t])
 
 
 def hand_over(*refs):
@@ -494,20 +586,24 @@
     dma = pltpu.SemaphoreType.DMA
     hbm = pl.BlockSpec(memory_space=pl.ANY)
     arrays = [
-        ((STEPS, 2, BLOCK, PAIR), bf16),
+        ((STEPS, 2, BLOCK, WIDE), bf16),
         ((SLOTS, 2, KEYS, HEAD_DIM), bf16),
         ((KEYS, 128), bf16),
         ((BLOCK, 128), bf16),
         ((HEAD_DIM, KEYS), bf16),
         ((2, KEYS, HEAD_DIM), f32),
         ((SLOTS, 2, BLOCK, HEAD_DIM), f32),
-        ((SPAN, PAIR), f32),
-        ((SPAN, PAIR), f32),
-        ((SPAN, PAIR), bf16),
-        ((SPAN, PAIR), bf16),
-        ((STEPS, BLOCK, PAIR), bf16),
-        ((SLOTS, BACK, 2, BLOCK, HEAD_DIM), bf16),
-        ((SLOTS, BACK, 2, BLOCK, HEAD_DIM), bf16),
+        ((SPAN, WIDE), f32),
+        ((SPAN, WIDE), f32),
+        ((SPAN, WIDE), bf16),
+        ((SPAN, GROUP), bf16),
+        ((SPAN, WIDE), f32),
+        ((SPAN, WIDE), f32),
+        ((SPAN, WIDE), bf16),
+        ((SPAN, GROUP), bf16),
+        ((STEPS, BLOCK, WIDE), bf16),
+        ((SLOTS, 2, BACK, BLOCK, HEAD_DIM), bf16),
+        ((SLOTS, 2, BACK, BLOCK, HEAD_DIM), bf16),
         ((SLOTS, 2, BLOCK, HEAD_DIM), bf16),
         ((SLOTS, 2, PREFIX, HEAD_DIM), bf16),
         ((BLOCKS, 2, PIECE, HEAD_DIM), bf16),
@@ -526,8 +622,8 @@
         STEPS,
         1,
         1,
-        SLOTS,
-        SLOTS,
+        (SLOTS, 2),
+        (SLOTS, 2),
         1,
         2,
         1,
@@ -549,7 +645,7 @@
         out_specs=(hbm,) * 5,
         scratch_shapes=[pltpu.VMEM(shape, kind) for shape, kind in arrays]
         + [pltpu.VMEM((64, 128), jnp.int32), pltpu.SMEM((SEGS,), jnp.int32)]
-        + [dma((size,)) for size in semaphores],
+        + [dma(size if isinstance(size, tuple) else (size,)) for size in semaphores],
         compiler_params=pltpu.CompilerParams(
             collective_id=0, has_side_effects=True, vmem_limit_bytes=56 * 1024 * 1024
         ),

time: 76.1 us -> 69.1 us (0.908)
  Pallas kernels: 74.8 us -> 68.3 us
    pallas_call x1, Pallas kernels: 72.5 us -> 66 us  [on_device(): pl.pallas_call(kernel, out_shape=results, in_specs=[hbm] * 8, out_specs=(...]
where the time goes in v3:
time: 69.1 us; the launch traced here: 68.9 us
  Pallas kernels  68.3 us (99%)
    pallas_call x1, Pallas kernels, on_device(): pl.pallas_call(kernel, out_shape=results, in_specs=[hbm] * 8, out_specs=(...  66 us
    pallas_call x1, Pallas kernels, on_device(): pl.pallas_call(hand_over, out_shape=results, in_specs=[hbm] * len(results...  2.32 us

profile of v3, /device:TPU:5, one launch (start us, length us, event | category | flops | bytes accessed | tf_op | source)
XLA Modules:
  0.0 68.9 jit_solution(13091096800419251168)
XLA Ops:
  0.6 66.0 %shard_map.119 = (bf16[64,8192]{1,0:T(8,128)(2,1)}, bf16[64,1024]{1,0:T(8,128)(2,1)}, bf16[64,1024]{1,0:T(8,128)(2,1)}, bf16[256,128]{1,0:T(8,128)(2,1)}, bf16[256,128]{1,0:T(8,128)(2,1)}) custom-call(bf16[64,8192]{1,0:T(8,128)(2,1)} %q.1, bf16[64,8192]{1,0:T(8,128)(2,1)} %g.1, bf16[64,1024]{1,0:T(8,128)(2,1)} %k.1, bf16[64,1024]{1,0:T(8,128)(2,1)} %v.1, ...), custom_call_target="tpu_custom_call" | custom-call | flops 7381975040 | bytes 4194304 | tf_op jit(solution)/shard_map/pallas_call | solution.py:641
  66.6 2.3 %shard_map.120 = (bf16[64,8192]{1,0:T(8,128)(2,1)}, bf16[64,1024]{1,0:T(8,128)(2,1)}, bf16[64,1024]{1,0:T(8,128)(2,1)}, bf16[256,128]{1,0:T(8,128)(2,1)}, bf16[256,128]{1,0:T(8,128)(2,1)}) custom-call(bf16[64,8192]{1,0:T(8,128)(2,1)} %get-tuple-element.10.refs_0_, bf16[64,1024]{1,0:T(8,128)(2,1)} %get-tuple-element.11.refs_1_, ...), custom_call_target="tpu_custom_call" | custom-call | tf_op jit(solution)/shard_map/pallas_call | solution.py:667

commit v4 on v3

--- a/solution.py
+++ b/solution.py
@@ -79,6 +79,7 @@
     dqb,
     part_out,
     part_in,
+    merge_in,
     own_out,
     pre_out,
     pre_in,
@@ -99,6 +100,7 @@
     dq_recv,
     part_send,
     part_recv,
+    merge_recv,
     own_send,
     own_recv,
     pre_send,
@@ -111,6 +113,8 @@
     y = lax.rem(h, RING)
     a = h // RING
     here = 2 * s + a
+    place = lax.rem(here, 4)
+    first_core = place < 2
 
     def at_y(j):
         return (s, RING * a + lax.rem(y + j, RING))
@@ -178,7 +182,12 @@
         src = kv.at[u, :, OWN:KEYS, :]
         dst = kv.at[u, :, OWN - d * BLOCK : KEYS - d * BLOCK, :]
         device = at_block(lax.rem(here + d, BLOCKS))
-        return remote(src, dst, win_send.at[u], win_recv.at[u], device)
+        return remote(src, dst, win_send.at[u], win_recv.at[u, (d - 1) // 2], device)
+
+    def win_share(u):
+        src = kv.at[u, :, OWN - 2 * BLOCK : OWN, :]
+        dst = kv.at[u, :, OWN - 4 * BLOCK : OWN - 2 * BLOCK, :]
+        return remote(src, dst, win_send.at[u], win_recv.at[u, 1], at_block(here + 2))
 
     def in_first(n, there):
         return (RING * (n // PARTS) + there) * GROUP + lax.rem(n, PARTS) * WIDE
@@ -210,6 +219,16 @@
             device,
         )
 
+    def merge_copy(u, t):
+        device = at_block(lax.rem(here + BLOCKS - 2, BLOCKS))
+        return remote(
+            part_out.at[u, t, 2:4],
+            merge_in.at[u, t],
+            part_send.at[u, t],
+            merge_recv.at[u, t],
+            device,
+        )
+
     def own_own(u, t):
         dst = (dk, dv)[t].at[:, columns((RING * u + y) * HEAD_DIM, HEAD_DIM)]
         return pltpu.make_async_copy(own_out.at[u, t, rows_of(y)], dst, own_recv.at[t])
@@ -261,8 +280,23 @@
 
     def send_windows(u):
         wait_for(kv.at[u, :, OWN:KEYS, :], kv_recv.at[u])
-        for d in steps_back:
-            win_copy(u, d).start()
+        win_copy(u, 1).start()
+        win_copy(u, 2).start()
+
+        @pl.when((place == 1) | (place == 2))
+        def _():
+            win_copy(u, 3).start()
+
+        @pl.when(first_core)
+        def _():
+            win_copy(u, 4).start()
+
+    def share_windows(u):
+        wait_for(kv.at[u, :, OWN - 2 * BLOCK : OWN, :], win_recv.at[u, 0])
+
+        @pl.when(first_core)
+        def _():
+            win_share(u).start()
 
     for t in range(2):
         for u in range(SLOTS):
@@ -274,6 +308,14 @@
 
     for copy in small:
         copy.wait()
+    @pl.when((place == 0) | (place == 3))
+    def _():
+        part_in[:, :, 2] = jnp.zeros((SLOTS, 2, BLOCK, HEAD_DIM), jnp.bfloat16)
+
+    @pl.when(jnp.logical_not(first_core))
+    def _():
+        part_in[:, :, 3] = jnp.zeros((SLOTS, 2, BLOCK, HEAD_DIM), jnp.bfloat16)
+
     documents = lax.broadcasted_iota(jnp.int32, (128, 128), 0)
     limits = jnp.zeros((128, 128), jnp.int32)
     for e in range(SEGS):
@@ -305,7 +347,7 @@
         send_in(n)
 
     def prepare(u):
-        wait_for(kv.at[u, :, PREFIX:OWN, :], win_recv.at[u])
+        wait_for(kv.at[u, :, PREFIX : OWN - 2 * BLOCK, :], win_recv.at[u, 1])
         for i in range(KEYS // 128):
             part = kv[u, 0, 128 * i : 128 * (i + 1), :].astype(jnp.float32)
             kt[:, 128 * i : 128 * (i + 1)] = part.T.astype(jnp.bfloat16)
@@ -450,10 +492,21 @@
 
     def close(u):
         for t in (1, 0):
-            for d in steps_back:
+            for d in (3, 4, 1, 2):
                 low = OWN - d * BLOCK
                 part_out[u, t, d - 1] = acc[t, low : low + BLOCK, :].astype(jnp.bfloat16)
-                part_copy(u, t, d).start()
+
+            @pl.when(first_core)
+            def _():
+                part_copy(u, t, 3).start()
+                part_copy(u, t, 4).start()
+
+            @pl.when(jnp.logical_not(first_core))
+            def _():
+                merge_copy(u, t).start()
+                part_copy(u, t, 1).start()
+                part_copy(u, t, 2).start()
+
         for t in range(2):
             pre_out[u, t] = acc[t, 0:PREFIX, :].astype(jnp.bfloat16)
             own_sum[u, t] = acc[t, OWN:KEYS, :]
@@ -472,9 +525,25 @@
 
         lax.fori_loop(1, SEQ, spread, 0)
 
+    def merge(u):
+        @pl.when(first_core)
+        def _():
+            for t in (1, 0):
+                wait_for(merge_in.at[u, t], merge_recv.at[u, t])
+                for d in (1, 2):
+                    both = part_out[u, t, d - 1].astype(jnp.float32)
+                    both += merge_in[u, t, d - 1].astype(jnp.float32)
+                    part_out[u, t, d - 1] = both.astype(jnp.bfloat16)
+                    part_copy(u, t, d).start()
+
     def finish(u):
         for t in (1, 0):
-            wait_for(part_in.at[u, t], part_recv.at[u, t])
+            for at, count in enumerate((3, 4, 3, 2)):
+
+                @pl.when(place == at)
+                def _():
+                    wait_for(part_in.at[u, t, 0:count], part_recv.at[u, t])
+
             whole = own_sum[u, t]
             for d in steps_back:
                 whole += part_in[u, t, d - 1].astype(jnp.float32)
@@ -508,6 +577,7 @@
         @pl.when(n == 0)
         def _():
             send_windows(1)
+            share_windows(0)
 
         @pl.when(lax.rem(n, PARTS) == 0)
         def _():
@@ -517,6 +587,10 @@
 
         attend(n, u)
 
+        @pl.when(n == PARTS - 1)
+        def _():
+            share_windows(1)
+
         @pl.when(lax.rem(n, PARTS) == PARTS - 1)
         def _():
             close(u)
@@ -524,6 +598,10 @@
         @pl.when(n == PARTS - 1)
         def _():
             query_part(0)
+
+        @pl.when(n == PARTS - 1)
+        def _():
+            merge(0)
 
         @pl.when(n == PARTS)
         def _():
@@ -534,6 +612,7 @@
 
     lax.fori_loop(0, STEPS, step, 0)
 
+    merge(1)
     query_part(1)
     hand_prefix(1)
     finish(1)
@@ -550,7 +629,12 @@
     wait_for(pre_out.at[0, :, 0 : PREFIX - PIECE], last_send.at[0])
     wait_for(pre_in.at[0 : BLOCKS - 1], pre_send.at[0])
     for u in range(SLOTS):
-        wait_for(kv.at[u, :, PREFIX:OWN, :], win_send.at[u])
+        for at, sent in enumerate((5, 6, 3, 2)):
+
+            @pl.when(place == at)
+            def _():
+                wait_for(kv.at[u, :, 0 : sent * BLOCK, :], win_send.at[u])
+
         for t in range(2):
             wait_for(part_out.at[u, t], part_send.at[u, t])
 
@@ -604,6 +688,7 @@
         ((STEPS, BLOCK, WIDE), bf16),
         ((SLOTS, 2, BACK, BLOCK, HEAD_DIM), bf16),
         ((SLOTS, 2, BACK, BLOCK, HEAD_DIM), bf16),
+        ((SLOTS, 2, 2, BLOCK, HEAD_DIM), bf16),
         ((SLOTS, 2, BLOCK, HEAD_DIM), bf16),
         ((SLOTS, 2, PREFIX, HEAD_DIM), bf16),
         ((BLOCKS, 2, PIECE, HEAD_DIM), bf16),
@@ -617,11 +702,12 @@
         1,
         1,
         SLOTS,
-        SLOTS,
+        (SLOTS, 2),
         2,
         STEPS,
         1,
         1,
+        (SLOTS, 2),
         (SLOTS, 2),
         (SLOTS, 2),
         1,

time: 69.1 us -> 62.7 us (0.907)
  Pallas kernels: 68.3 us -> 61.9 us
    pallas_call x1, Pallas kernels: 66 us -> 59.6 us  [on_device(): pl.pallas_call(kernel, out_shape=results, in_specs=[hbm] * 8, out_specs=(...]
where the time goes in v4:
time: 62.7 us; the launch traced here: 62.5 us
  Pallas kernels  61.9 us (99%)
  between operations  0.64 us (1%)
    pallas_call x1, Pallas kernels, on_device(): pl.pallas_call(kernel, out_shape=results, in_specs=[hbm] * 8, out_specs=(...  59.6 us
    pallas_call x1, Pallas kernels, on_device(): pl.pallas_call(hand_over, out_shape=results, in_specs=[hbm] * len(results...  2.32 us

profile of v4, /device:TPU:5, one launch (start us, length us, event | category | flops | bytes accessed | tf_op | source)
XLA Modules:
  0.0 62.5 jit_solution(1685250708529153432)
XLA Ops:
  0.6 59.6 %shard_map.119 = (bf16[64,8192]{1,0:T(8,128)(2,1)}, bf16[64,1024]{1,0:T(8,128)(2,1)}, bf16[64,1024]{1,0:T(8,128)(2,1)}, bf16[256,128]{1,0:T(8,128)(2,1)}, bf16[256,128]{1,0:T(8,128)(2,1)}) custom-call(bf16[64,8192]{1,0:T(8,128)(2,1)} %q.1, bf16[64,8192]{1,0:T(8,128)(2,1)} %g.1, bf16[64,1024]{1,0:T(8,128)(2,1)} %k.1, bf16[64,1024]{1,0:T(8,128)(2,1)} %v.1, ...), custom_call_target="tpu_custom_call" | custom-call | flops 7381975040 | bytes 4194304 | tf_op jit(solution)/shard_map/pallas_call | solution.py:727
  60.2 2.3 %shard_map.120 = (bf16[64,8192]{1,0:T(8,128)(2,1)}, bf16[64,1024]{1,0:T(8,128)(2,1)}, bf16[64,1024]{1,0:T(8,128)(2,1)}, bf16[256,128]{1,0:T(8,128)(2,1)}, bf16[256,128]{1,0:T(8,128)(2,1)}) custom-call(bf16[64,8192]{1,0:T(8,128)(2,1)} %get-tuple-element.10.refs_0_, bf16[64,1024]{1,0:T(8,128)(2,1)} %get-tuple-element.11.refs_1_, ...), custom_call_target="tpu_custom_call" | custom-call | tf_op jit(solution)/shard_map/pallas_call | solution.py:753

commit v5 on v4

--- a/solution.py
+++ b/solution.py
@@ -178,6 +178,10 @@
             (pk, pv)[t], kv.at[a, t, 0:PREFIX], fix_send.at[0], fix_recv.at[0], device
         )
 
+    def fix_share():
+        ref = kv.at[1 - a, :, 0:PREFIX]
+        return remote(ref, ref, fix_send.at[0], fix_recv.at[0], at_block(here + 2))
+
     def win_copy(u, d):
         src = kv.at[u, :, OWN:KEYS, :]
         dst = kv.at[u, :, OWN - d * BLOCK : KEYS - d * BLOCK, :]
@@ -337,8 +341,11 @@
 
     pl.semaphore_wait(barrier, RING - 1 + BLOCKS - 1)
     send_kv(0)
-    for t in range(2):
-        fix_copy(t).start()
+    @pl.when(first_core)
+    def _():
+        for t in range(2):
+            fix_copy(t).start()
+
     send_in(0)
     send_kv(1)
 
@@ -474,8 +481,10 @@
         for do in gather_up(1, first, *held[1]):
             do()
 
-    def query_part(u):
+    def query_part(u, between=None):
         for i in range(2):
+            if i == 1 and between is not None:
+                between(u)
             _, _, _, ds_ref = passes[i]
             rows = pl.ds(SUB * i, SUB)
             near = pl.ds(PREFIX + SUB * i, NEAR)
@@ -571,13 +580,18 @@
     wait_for(kv.at[0, :, 0:PREFIX], fix_local.at[0])
     wait_for(kv.at[0, :, 0:PREFIX], fix_recv.at[0])
 
+    @pl.when(first_core)
+    def _():
+        fix_share().start()
+
+
     def step(n, carry):
         u = n // PARTS
 
         @pl.when(n == 0)
         def _():
+            share_windows(0)
             send_windows(1)
-            share_windows(0)
 
         @pl.when(lax.rem(n, PARTS) == 0)
         def _():
@@ -612,8 +626,7 @@
 
     lax.fori_loop(0, STEPS, step, 0)
 
-    merge(1)
-    query_part(1)
+    query_part(1, merge)
     hand_prefix(1)
     finish(1)
 
@@ -625,7 +638,10 @@
     wait_for(dq, dq_recv.at[0])
     wait_for(own_out.at[:, :, 0 : BLOCK - ROWS], kv_send.at[0])
     wait_for(own_out.at[:, :, 0 : BLOCK - ROWS], own_send.at[0])
-    wait_for(pre_out.at[0], fix_send.at[0])
+    @pl.when(first_core)
+    def _():
+        wait_for(pre_out, fix_send.at[0])
+
     wait_for(pre_out.at[0, :, 0 : PREFIX - PIECE], last_send.at[0])
     wait_for(pre_in.at[0 : BLOCKS - 1], pre_send.at[0])
     for u in range(SLOTS):

time: 62.7 us -> 61.1 us (0.974)
  Pallas kernels: 61.9 us -> 60.2 us
    pallas_call x1, Pallas kernels: 59.6 us -> 57.9 us  [on_device(): pl.pallas_call(kernel, out_shape=results, in_specs=[hbm] * 8, out_specs=(...]
where the time goes in v5:
time: 61.1 us; the launch traced here: 60.9 us
  Pallas kernels  60.2 us (99%)
  between operations  0.64 us (1%)
    pallas_call x1, Pallas kernels, on_device(): pl.pallas_call(kernel, out_shape=results, in_specs=[hbm] * 8, out_specs=(...  57.9 us
    pallas_call x1, Pallas kernels, on_device(): pl.pallas_call(hand_over, out_shape=results, in_specs=[hbm] * len(results...  2.32 us

profile of v5, /device:TPU:5, one launch (start us, length us, event | category | flops | bytes accessed | tf_op | source)
XLA Modules:
  0.0 60.9 jit_solution(4885275227199455403)
XLA Ops:
  0.6 57.9 %shard_map.119 = (bf16[64,8192]{1,0:T(8,128)(2,1)}, bf16[64,1024]{1,0:T(8,128)(2,1)}, bf16[64,1024]{1,0:T(8,128)(2,1)}, bf16[256,128]{1,0:T(8,128)(2,1)}, bf16[256,128]{1,0:T(8,128)(2,1)}) custom-call(bf16[64,8192]{1,0:T(8,128)(2,1)} %q.1, bf16[64,8192]{1,0:T(8,128)(2,1)} %g.1, bf16[64,1024]{1,0:T(8,128)(2,1)} %k.1, bf16[64,1024]{1,0:T(8,128)(2,1)} %v.1, ...), custom_call_target="tpu_custom_call" | custom-call | flops 7381975040 | bytes 4194304 | tf_op jit(solution)/shard_map/pallas_call | solution.py:743
  58.5 2.3 %shard_map.120 = (bf16[64,8192]{1,0:T(8,128)(2,1)}, bf16[64,1024]{1,0:T(8,128)(2,1)}, bf16[64,1024]{1,0:T(8,128)(2,1)}, bf16[256,128]{1,0:T(8,128)(2,1)}, bf16[256,128]{1,0:T(8,128)(2,1)}) custom-call(bf16[64,8192]{1,0:T(8,128)(2,1)} %get-tuple-element.10.refs_0_, bf16[64,1024]{1,0:T(8,128)(2,1)} %get-tuple-element.11.refs_1_, ...), custom_call_target="tpu_custom_call" | custom-call | tf_op jit(solution)/shard_map/pallas_call | solution.py:769

commit v6 on v5

--- a/solution.py
+++ b/solution.py
@@ -500,6 +500,23 @@
             dq_own(PARTS * u + n).start()
 
     def close(u):
+        for t in range(2):
+            pre_out[u, t] = acc[t, 0:PREFIX, :].astype(jnp.bfloat16)
+
+        @pl.when(a == u)
+        def _():
+            pre_in[here] = pre_out[u, :, piece_rows(s), :]
+
+        @pl.when(a != u)
+        def _():
+            pre_copy(u, 0).start()
+
+        def spread(i, carry):
+            pre_copy(u, i).start()
+            return carry
+
+        lax.fori_loop(1, SEQ, spread, 0)
+
         for t in (1, 0):
             for d in (3, 4, 1, 2):
                 low = OWN - d * BLOCK
@@ -517,22 +534,8 @@
                 part_copy(u, t, 2).start()
 
         for t in range(2):
-            pre_out[u, t] = acc[t, 0:PREFIX, :].astype(jnp.bfloat16)
             own_sum[u, t] = acc[t, OWN:KEYS, :]
 
-        @pl.when(a == u)
-        def _():
-            pre_in[here] = pre_out[u, :, piece_rows(s), :]
-
-        @pl.when(a != u)
-        def _():
-            pre_copy(u, 0).start()
-
-        def spread(i, carry):
-            pre_copy(u, i).start()
-            return carry
-
-        lax.fori_loop(1, SEQ, spread, 0)
 
     def merge(u):
         @pl.when(first_core)

time: 61.1 us -> 60.2 us (0.985)
  Pallas kernels: 60.2 us -> 59.3 us
    pallas_call x1, Pallas kernels: 57.9 us -> 57 us  [on_device(): pl.pallas_call(kernel, out_shape=results, in_specs=[hbm] * 8, out_specs=(...]
where the time goes in v6:
time: 60.2 us; the launch traced here: 60 us
  Pallas kernels  59.3 us (99%)
  between operations  0.64 us (1%)
    pallas_call x1, Pallas kernels, on_device(): pl.pallas_call(kernel, out_shape=results, in_specs=[hbm] * 8, out_specs=(...  57 us
    pallas_call x1, Pallas kernels, on_device(): pl.pallas_call(hand_over, out_shape=results, in_specs=[hbm] * len(results...  2.32 us

profile of v6, /device:TPU:5, one launch (start us, length us, event | category | flops | bytes accessed | tf_op | source)
XLA Modules:
  0.0 60.0 jit_solution(13647442360508699346)
XLA Ops:
  0.6 57.0 %shard_map.119 = (bf16[64,8192]{1,0:T(8,128)(2,1)}, bf16[64,1024]{1,0:T(8,128)(2,1)}, bf16[64,1024]{1,0:T(8,128)(2,1)}, bf16[256,128]{1,0:T(8,128)(2,1)}, bf16[256,128]{1,0:T(8,128)(2,1)}) custom-call(bf16[64,8192]{1,0:T(8,128)(2,1)} %q.1, bf16[64,8192]{1,0:T(8,128)(2,1)} %g.1, bf16[64,1024]{1,0:T(8,128)(2,1)} %k.1, bf16[64,1024]{1,0:T(8,128)(2,1)} %v.1, ...), custom_call_target="tpu_custom_call" | custom-call | flops 7381975040 | bytes 4194304 | tf_op jit(solution)/shard_map/pallas_call | solution.py:746
  57.6 2.3 %shard_map.120 = (bf16[64,8192]{1,0:T(8,128)(2,1)}, bf16[64,1024]{1,0:T(8,128)(2,1)}, bf16[64,1024]{1,0:T(8,128)(2,1)}, bf16[256,128]{1,0:T(8,128)(2,1)}, bf16[256,128]{1,0:T(8,128)(2,1)}) custom-call(bf16[64,8192]{1,0:T(8,128)(2,1)} %get-tuple-element.10.refs_0_, bf16[64,1024]{1,0:T(8,128)(2,1)} %get-tuple-element.11.refs_1_, ...), custom_call_target="tpu_custom_call" | custom-call | tf_op jit(solution)/shard_map/pallas_call | solution.py:772
